TPU v7x, 256 devices: a whole 4x4x8 slice. The times are simulated.
256 devices in a mesh: bins: 32 (over x, z), samp: 8 (over y, core).
Axes of the slice: x: 4, y: 4, z: 8, core: 2. Of those that a mesh axis runs over, the one named last changes fastest.
Arguments:
- signal: float32 [2048, 32768], P('samp', 'bins'), may hold values from -6 to 6
- jumps: float32 [2048, 1024], P('samp', 'bins'), as said below
- breaks: int32 [1024], P('bins'), may hold values from 0 to 32766, as said below
Outputs:
- residual: float32 [2048, 32768], P('samp', 'bins')
- jumps_out: float32 [2048, 1024], P('samp', 'bins')
Inputs may be any that keep to these rules, and one draw needn't show every extreme that they name: Entries 32 * d to 32 * (d + 1) - 1 of breaks lie in bins d * 1024 to (d + 1) * 1024 - 2; entries may repeat; the first breakpoint is at bin 0 and the last at bin 32768 - 2. `jumps`: jumps of different breakpoints have different scales.
All inputs are finite; a program needn't handle non-finite values.
Results may differ from a plain program's by a relative error of at most 0.00011.
Values sent between devices are 32-bit elements; how exact they have to be, the bound alone decides.
No kernel may reach another device: no remote copies, remote signals or barrier semaphores. Data moves between devices by JAX's collectives and lax.ppermute only.
A program may use at most 64 MiB of HBM per device.

v0:
```python
import jax
import jax.numpy as jnp
from jax import lax
from jax.sharding import PartitionSpec as P

PASSES = 2


epsilon = 1e-06
shrink_level = 0.5


def entering(value, axis, join, neutral):
    count, mine = (lax.axis_size(axis), lax.axis_index(axis))
    pieces = lax.all_gather(value, axis)
    pieces = pieces[::-1]
    mine = count - 1 - mine
    subtotal = jnp.full_like(value, 0) + jnp.asarray(neutral, value.dtype)

    def lap(position, subtotal):
        longer = join(subtotal, pieces[position])
        return jnp.where(position < mine, longer, subtotal)

    return lax.fori_loop(0, count - 1, lap, subtotal)


def add_pair(earlier, later):
    return earlier + later


def body(signal, jumps, breaks):
    slab_index = lax.axis_index("bins")
    slab_width = signal.shape[1]
    jump_count = jumps.shape[1]
    sample_rows = signal.shape[0]
    local_pos = breaks - slab_index * slab_width
    bin_iota = lax.broadcasted_iota(jnp.int32, (jump_count, slab_width), 1)
    below_mask = (local_pos[:, None] < bin_iota).astype(jnp.float32)
    after_mask = (bin_iota > local_pos[:, None]).astype(jnp.float32)

    def steps_of(amounts):
        inside = jnp.dot(amounts, below_mask, precision=lax.Precision.HIGHEST)
        empty = jnp.zeros((sample_rows,), jnp.float32)
        shard_part = lax.all_gather(amounts, "bins", axis=1, tiled=True)
        columns = lax.broadcasted_iota(jnp.int32, shard_part.shape, 1)
        before = columns < slab_index * jump_count
        left_carry = empty + jnp.sum(jnp.where(before, shard_part, 0.0), axis=1)
        return inside + left_carry[:, None]

    resid = signal - steps_of(jumps)
    jumps_now = jumps
    for step_num in range(PASSES):
        slab_total = jnp.sum(resid, axis=1)
        right_carry = entering(slab_total, "bins", add_pair, jnp.zeros((sample_rows,), jnp.float32))
        after_breaks = jnp.dot(resid, after_mask.T, precision=lax.Precision.HIGHEST)
        corr = right_carry[:, None] + after_breaks
        grad_sum = lax.psum(jnp.sum(corr * corr), ("bins", "samp"))
        image = steps_of(corr)
        curv_sum = lax.psum(jnp.sum(image * image), ("bins", "samp"))
        step_size = grad_sum / (curv_sum + epsilon)
        moved = jumps_now + step_size * corr
        group_sq = lax.psum(jnp.sum(moved * moved, axis=0), "samp")
        group_norm = jnp.sqrt(group_sq + epsilon)
        norm_total = lax.psum(jnp.sum(group_norm), "bins")
        level_mean = norm_total / (jump_count * lax.axis_size("bins"))
        shrunk = moved * jnp.maximum(0.0, 1.0 - shrink_level * level_mean / group_norm)
        resid = resid - steps_of(shrunk - jumps_now)
        jumps_now = shrunk
    return (resid, jumps_now)


def solution(mesh):
    return jax.shard_map(
        body,
        mesh=mesh,
        in_specs=(P("samp", "bins"), P("samp", "bins"), P("bins")),
        out_specs=(P("samp", "bins"), P("samp", "bins")),
        check_vma=False,
    )
```

profile of v0, /device:TPU:1, one launch (start us, length us, event | category | flops | bytes accessed | tf_op | source)
XLA Modules:
  0.0 806.4 jit_solution(10502231201398969155)
XLA Ops:
  8.0 1.6 copy.9
  10.2 76.0 %all-gather.10.cloned.1.call-done = f32[256,1024]{0,1:T(8,128)} async-done(((f32[256,32]{0,1:T(8,128)}), f32[256,1024]{0,1:T(8,128)}) %all-gather.10.cloned.1.call-update) | async-done | bytes 1048592 | tf_op jit(solution)/shard_map/all_gather | solution.py:44
  86.1 1.4 select_reduce_fusion.4
  88.3 30.8 %all-gather.2 = f32[32,1,256]{2,1,0:T(1,128)S(1)} all-gather(f32[1,1,256]{2,1,0:T(1,128)S(1)} %bitcast.30), channel_id=2, replica_groups=mesh['bins'=32,'samp'=8] {'bins'}, dimensions={0}, use_global_device_ids=true | all-gather | bytes 33792 | tf_op jit(solution)/shard_map/all_gather | solution.py:15
  119.2 1.7 while.28
  120.9 1.8 multiply_reduce_fusion.3
  122.8 85.0 %all-gather.12.cloned.1.call-done = f32[256,1024]{0,1:T(8,128)} async-done(((f32[256,32]{0,1:T(8,128)}), f32[256,1024]{0,1:T(8,128)}) %all-gather.12.cloned.1.call-update) | async-done | bytes 1048592 | tf_op jit(solution)/shard_map/all_gather | solution.py:44
  207.8 1.4 select_reduce_fusion.3
  209.2 1.4 fusion.6
  210.6 78.8 %all-reduce.1 = (f32[]{:T(128)}, f32[]{:T(128)}) all-reduce(f32[]{:T(128)} %get-tuple-element.222, f32[]{:T(128)} %fusion.6), channel_id=1, replica_groups=mesh['bins'=32,'samp'=8] {'bins','samp'}, use_global_device_ids=true, to_apply=%region_5.6 | all-reduce | flops 2 | bytes 16 | tf_op jit(solution)/shard_map/psum | solution.py:57
  290.9 12.4 %psum.58 = f32[32]{0:T(128)S(1)} all-reduce(f32[32]{0:T(128)S(1)} %get-tuple-element.218), channel_id=1, replica_groups=mesh['bins'=32,'samp'=8] {'samp'}, use_global_device_ids=true, to_apply=%region_10.11 | all-reduce | flops 32 | bytes 256 | tf_op jit(solution)/shard_map/psum | solution.py:62
  304.0 58.3 %psum.59 = f32[]{:T(128)} all-reduce(f32[]{:T(128)} %fusion.15), channel_id=1, replica_groups=mesh['bins'=32,'samp'=8] {'bins'}, use_global_device_ids=true, to_apply=%region_12.13 | all-reduce | flops 1 | bytes 8 | tf_op jit(solution)/shard_map/psum | solution.py:64
  363.7 77.6 %all-gather.14.cloned.1.call-done = f32[256,1024]{0,1:T(8,128)} async-done(((f32[256,32]{0,1:T(8,128)}), f32[256,1024]{0,1:T(8,128)}) %all-gather.14.cloned.1.call-update) | async-done | bytes 1048592 | tf_op jit(solution)/shard_map/all_gather | solution.py:44
  441.3 1.4 select_reduce_fusion.2
  443.5 30.8 %all-gather.3 = f32[32,1,256]{2,1,0:T(1,128)S(1)} all-gather(f32[1,1,256]{2,1,0:T(1,128)S(1)} %bitcast.29), channel_id=3, replica_groups=mesh['bins'=32,'samp'=8] {'bins'}, dimensions={0}, use_global_device_ids=true | all-gather | bytes 33792 | tf_op jit(solution)/shard_map/all_gather | solution.py:15
  474.4 1.7 while.29
  476.0 1.7 multiply_reduce_fusion.1
  477.9 85.0 %all-gather.16.cloned.1.call-done = f32[256,1024]{0,1:T(8,128)} async-done(((f32[256,32]{0,1:T(8,128)}), f32[256,1024]{0,1:T(8,128)}) %all-gather.16.cloned.1.call-update) | async-done | bytes 1048592 | tf_op jit(solution)/shard_map/all_gather | solution.py:44
  562.9 1.4 select_reduce_fusion.1
  565.7 78.8 %all-reduce = (f32[]{:T(128)}, f32[]{:T(128)}) all-reduce(f32[]{:T(128)} %get-tuple-element.226, f32[]{:T(128)} %fusion.7), channel_id=1, replica_groups=mesh['bins'=32,'samp'=8] {'bins','samp'}, use_global_device_ids=true, to_apply=%region_18.19 | all-reduce | flops 2 | bytes 16 | tf_op jit(solution)/shard_map/psum | solution.py:57
  646.0 12.4 %psum.62 = f32[32]{0:T(128)S(1)} all-reduce(f32[32]{0:T(128)S(1)} %multiply_reduce_fusion), channel_id=1, replica_groups=mesh['bins'=32,'samp'=8] {'samp'}, use_global_device_ids=true, to_apply=%region_23.24 | all-reduce | flops 32 | bytes 256 | tf_op jit(solution)/shard_map/psum | solution.py:62
  659.1 58.3 %psum.63 = f32[]{:T(128)} all-reduce(f32[]{:T(128)} %fusion.16), channel_id=1, replica_groups=mesh['bins'=32,'samp'=8] {'bins'}, use_global_device_ids=true, to_apply=%region_25.26 | all-reduce | flops 1 | bytes 8 | tf_op jit(solution)/shard_map/psum | solution.py:64
  718.8 77.6 %all-gather.18.cloned.1.call-done = f32[256,1024]{0,1:T(8,128)} async-done(((f32[256,32]{0,1:T(8,128)}), f32[256,1024]{0,1:T(8,128)}) %all-gather.18.cloned.1.call-update) | async-done | bytes 1048592 | tf_op jit(solution)/shard_map/all_gather | solution.py:44
  796.4 1.4 select_reduce_fusion
  (167 shorter events, 10.9 us)
Async XLA Ops:
  7.2 79.0 %all-gather.10.cloned.1.call-start = ((), (), s32[]{:S(2)}) async-start(), calls=%async_computation | async-start | bytes 1081344 | tf_op jit(solution)/shard_map/all_gather | solution.py:44
  7.9 199.9 %all-gather.12.cloned.1.call-start = ((), (), s32[]{:S(2)}) async-start(), calls=%async_computation.1 | async-start | bytes 1081344 | tf_op jit(solution)/shard_map/all_gather | solution.py:44
  9.5 0.7 copy-start.5
  10.2 77.4 %copy-start = (f32[256,32]{0,1:T(8,128)S(1)}, f32[256,32]{0,1:T(8,128)}, u32[]{:S(2)}) copy-start(f32[256,32]{0,1:T(8,128)} %param.8) | copy-start | bytes 98308
  122.7 86.5 %copy-start.4 = (f32[256,32]{0,1:T(8,128)S(1)}, f32[256,32]{0,1:T(8,128)}, u32[]{:S(2)}) copy-start(f32[256,32]{0,1:T(8,128)} %get-tuple-element.223) | copy-start | bytes 98308
  122.7 318.6 %all-gather.14.cloned.1.call-start = ((), (), s32[]{:S(2)}) async-start(), calls=%async_computation.2 | async-start | bytes 1081344 | tf_op jit(solution)/shard_map/all_gather | solution.py:44
  363.7 199.2 %all-gather.16.cloned.1.call-start = ((), (), s32[]{:S(2)}) async-start(), calls=%async_computation.3 | async-start | bytes 1081344 | tf_op jit(solution)/shard_map/all_gather | solution.py:44
  363.7 79.0 %copy-start.2 = (f32[256,32]{0,1:T(8,128)S(1)}, f32[256,32]{0,1:T(8,128)}, u32[]{:S(2)}) copy-start(f32[256,32]{0,1:T(8,128)} %multiply_subtract_fusion.1) | copy-start | bytes 98308
  477.8 86.5 %copy-start.1 = (f32[256,32]{0,1:T(8,128)S(1)}, f32[256,32]{0,1:T(8,128)}, u32[]{:S(2)}) copy-start(f32[256,32]{0,1:T(8,128)} %get-tuple-element.227) | copy-start | bytes 98308
  477.8 318.6 %all-gather.18.cloned.1.call-start = ((), (), s32[]{:S(2)}) async-start(), calls=%async_computation.4 | async-start | bytes 1081344 | tf_op jit(solution)/shard_map/all_gather | solution.py:44
  718.8 79.1 %copy-start.3 = (f32[256,32]{0,1:T(8,128)S(1)}, f32[256,32]{0,1:T(8,128)}, u32[]{:S(2)}) copy-start(f32[256,32]{0,1:T(8,128)} %get-tuple-element.216) | copy-start | bytes 98308
Sparse Core Ops, SparseCore 0:
  10.6 75.5 all-gather.9
  122.8 84.9 all-gather.11
  363.8 77.4 all-gather.13
  477.9 84.9 all-gather.15
  718.9 77.4 all-gather.17
where the time goes:
time: 811 us; the launch traced here: 806 us
  waiting for transfers between devices  402 us (50%)
  blocking collectives  361 us (45%)
  between operations  17.9 us (2%)
  other arithmetic  10.9 us (1%)
  matrix products  8.4 us (1%)
    all_gather x5, waiting for transfers between devices, steps_of(): shard_part = lax.all_gather(amounts, 'bins', axis=1, tiled=True)  401 us
    psum x2, blocking collectives, body(): grad_sum = lax.psum(jnp.sum(corr * corr), ('bins', 'samp'))  158 us
    psum x2, blocking collectives, body(): norm_total = lax.psum(jnp.sum(group_norm), 'bins')  117 us
    all_gather x2, blocking collectives, entering(): pieces = lax.all_gather(value, axis)  61.7 us
    psum x2, blocking collectives, body(): group_sq = lax.psum(jnp.sum(moved * moved, axis=0), 'samp')  24.9 us
  transfers between devices with their start and end apart: 5, of which 5 were waited for; matrix products, arithmetic and copies ran while one was open for 0% of the time, Pallas kernels for 0%

commit v1 on v0

v1 whole, which is shorter than its diff:
```python
import functools

import jax
import jax.numpy as jnp
from jax import lax
from jax.experimental import pallas as pl
from jax.experimental.pallas import tpu as pltpu
from jax.sharding import Mesh, PartitionSpec as P

EPS = 1e-06
SHRINK = 0.5
NX, NZ, NY, NC = 4, 8, 4, 2
KD = 32
KZ = KD * NZ
F32 = jnp.float32
BF16 = jnp.bfloat16
VMEM = pl.BlockSpec(memory_space=pltpu.VMEM)
SMEM = pl.BlockSpec(memory_space=pltpu.SMEM)


def pieces(v):
    hi = v.astype(BF16)
    rest = v - hi.astype(F32)
    mid = rest.astype(BF16)
    low = (rest - mid.astype(F32)).astype(BF16)
    return hi, mid, low


def dot(a, b):
    return jnp.dot(a, b, precision=lax.Precision.HIGHEST, preferred_element_type=F32)


def call(kernel, out_shape, n_in, smem=0, limit=32):
    n_out = len(out_shape)
    return pl.pallas_call(
        kernel,
        out_shape=[jax.ShapeDtypeStruct(s, F32) for s in out_shape],
        in_specs=[SMEM] * smem + [VMEM] * (n_in - smem),
        out_specs=[VMEM] * n_out,
        compiler_params=pltpu.CompilerParams(vmem_limit_bytes=limit << 20),
    )


def local_sums(breaks, signal, jumps, out):
    rows, width = signal.shape
    z = lax.axis_index("z")
    start = (lax.axis_index("x") * NZ + z) * width
    sub = lax.broadcasted_iota(jnp.int32, (40, 128), 0)
    lane = lax.broadcasted_iota(jnp.int32, (8, KZ), 1)
    at = jnp.where(sub == KD, -1, width)
    row = jnp.zeros((8, KZ), jnp.int32)
    for k in range(KD):
        at = jnp.where(sub == k, breaks[k] - start, at)
        row = jnp.where(lane == z * KD + k, breaks[k], row)
    at = jnp.concatenate([at] * (width // 128), axis=1)
    mask = (lax.broadcasted_iota(jnp.int32, (40, width), 1) > at).astype(BF16)
    total = jnp.zeros((40, rows), F32)
    for piece in pieces(signal[...])[::-1]:
        total += lax.dot_general(mask, piece, (((1,), (1,)), ((), ())), preferred_element_type=F32)
    out[0:KD, :] = jumps[...].T
    out[KD : 2 * KD, :] = total[:KD]
    sub8 = lax.broadcasted_iota(jnp.int32, (8, KZ), 0)
    out[2 * KD :, :] = jnp.where(sub8 == 1, row.astype(F32), total[KD:])


def gram(after):
    wide = jnp.broadcast_to(after, (KZ, KZ))
    return jnp.minimum(wide, wide.T), wide


def group_sums(bins, got, out):
    head = got[...]
    marks = jnp.sum(head[:, 2 * KD + 1, :], axis=0, keepdims=True)
    after = (bins - 1.0) - marks
    overlap, wide = gram(after)
    jumps = head[:, :KD, :].reshape(KZ, KZ)
    later = jnp.zeros((1, KZ), F32)
    behind = [None] * NZ
    for z in range(NZ - 1, -1, -1):
        behind[z] = head[z, KD : 2 * KD, :] + later
        later = later + head[z, 2 * KD : 2 * KD + 1, :]
    corr = jnp.concatenate(behind, axis=0) - dot(overlap, jumps)
    out[0:KZ, :] = jumps.T
    out[KZ : 2 * KZ, :] = corr.T
    out[2 * KZ : 2 * KZ + 1, :] = later
    out[2 * KZ + 1 : 2 * KZ + 2, :] = jnp.sum(jumps, axis=0, keepdims=True)
    out[2 * KZ + 2 : 2 * KZ + 3, :] = jnp.sum(jumps * wide.T, axis=0, keepdims=True)
    out[2 * KZ + 3 : 2 * KZ + 4, :] = after
    out[2 * KZ + 4 :, :] = jnp.zeros((4, KZ), F32)


def places():
    x = lax.axis_index("x")
    return [lax.rem(x + NX - k, NX) for k in range(NX)]


def carries(place, lower, upper):
    before, behind = [], []
    for p in range(NX):
        a, b = 0.0, 0.0
        for q in range(NX):
            if q != p:
                a = a + jnp.where(place[q] < place[p], lower[q], 0.0)
                b = b + jnp.where(place[q] > place[p], upper[q], 0.0)
        before.append(a)
        behind.append(b)
    return before, behind


def write_stats(stats, place, jumps, corr, after, overlap):
    sums, weighted = [], []
    for p in range(NX):
        c, j = corr[p], jumps[p]
        sums.append(jnp.sum(c, axis=1, keepdims=True))
        weighted.append(jnp.sum(c * after[p], axis=1, keepdims=True))
        stats[3 * p : 3 * p + 1, :] = jnp.sum(j * j, axis=0, keepdims=True)
        stats[3 * p + 1 : 3 * p + 2, :] = jnp.sum(j * c, axis=0, keepdims=True)
        stats[3 * p + 2 : 3 * p + 3, :] = jnp.sum(c * c, axis=0, keepdims=True)
    before, _ = carries(place, sums, weighted)
    curv = jnp.zeros((1, KZ), F32)
    cross = jnp.zeros((KZ, 1), F32)
    for p in range(NX):
        curv += jnp.sum(corr[p] * dot(corr[p], overlap[p]), axis=0, keepdims=True)
        cross += weighted[p] * before[p]
    lane = lax.broadcasted_iota(jnp.int32, (1, KZ), 1)
    curv += jnp.where(lane == 0, 2.0 * jnp.sum(cross), 0.0)
    stats[3 * NX : 3 * NX + 1, :] = curv
    stats[3 * NX + 1 :, :] = jnp.zeros((3, KZ), F32)


def first_corr(g0, g1, g2, g3, corr_out, stats):
    place = places()
    groups = (g0, g1, g2, g3)
    row = lambda p, k: groups[p][2 * KZ + k : 2 * KZ + k + 1, :]
    after = [row(p, 3) for p in range(NX)]
    overlap = [gram(a)[0] for a in after]
    before, behind = carries(place, [row(p, 1) for p in range(NX)], [row(p, 0) - row(p, 2) for p in range(NX)])
    columns = jnp.concatenate(before + behind, axis=0).T
    corr = []
    for p in range(NX):
        c = groups[p][KZ : 2 * KZ, :] + columns[:, NX + p : NX + p + 1] - columns[:, p : p + 1] * after[p]
        corr_out[p] = c
        corr.append(c)
    write_stats(stats, place, [g[0:KZ, :] for g in groups], corr, after, overlap)


def shrink_of(parts):
    total = (parts[0][...] + parts[1][...]) + (parts[2][...] + parts[3][...])
    grad = 0.0
    for p in range(NX):
        grad = grad + total[3 * p + 2 : 3 * p + 3, :]
    curv = total[3 * NX : 3 * NX + 1, :]
    step = jnp.sum(grad, axis=1, keepdims=True) / (jnp.sum(curv, axis=1, keepdims=True) + EPS)
    norms, level = [], 0.0
    for p in range(NX):
        jj, jc, cc = (total[3 * p + k : 3 * p + k + 1, :] for k in range(3))
        square = jj + 2.0 * step * jc + step * step * cc
        norms.append(jnp.sqrt(jnp.maximum(square, 0.0) + EPS))
        level = level + norms[-1]
    level = jnp.sum(level, axis=1, keepdims=True) / (NX * KZ)
    return step, [jnp.maximum(0.0, 1.0 - SHRINK * level / n) for n in norms]


def second_corr(g0, g1, g2, g3, corr_in, s0, s1, s2, s3, jumps_out, corr_out, stats):
    place = places()
    groups = (g0, g1, g2, g3)
    after = [g[2 * KZ + 3 : 2 * KZ + 4, :] for g in groups]
    overlap = [gram(a)[0] for a in after]
    step, factor = shrink_of((s0, s1, s2, s3))
    jumps, change, sums, weighted = [], [], [], []
    for p in range(NX):
        j = groups[p][0:KZ, :]
        new = factor[p] * (j + step * corr_in[p])
        d = new - j
        jumps_out[p] = new
        jumps.append(new)
        change.append(d)
        sums.append(jnp.sum(d, axis=1, keepdims=True))
        weighted.append(jnp.sum(d * after[p], axis=1, keepdims=True))
    before, behind = carries(place, sums, weighted)
    corr = []
    for p in range(NX):
        c = corr_in[p] - dot(change[p], overlap[p]) - before[p] * after[p] - behind[p]
        corr_out[p] = c
        corr.append(c)
    write_stats(stats, place, jumps, corr, after, overlap)


def finish(bins, signal, g0, jumps_in, corr_in, s0, s1, s2, s3, resid, jumps_out):
    place = places()
    z = lax.axis_index("z")
    width = signal.shape[1]
    step, factor = shrink_of((s0, s1, s2, s3))
    left = jnp.zeros((KZ, KZ), F32)
    for p in range(NX - 1, -1, -1):
        new = factor[p] * (jumps_in[p] + step * corr_in[p])
        if p:
            left += jnp.where(place[p] < place[0], new, 0.0)
    left = jnp.sum(left, axis=1, keepdims=True)
    marks = (bins - 1.0) - g0[2 * KZ + 3 : 2 * KZ + 4, :]
    wide = jnp.broadcast_to(marks, (KZ, KZ)).T
    start = ((place[0] * NZ + z) * width).astype(F32)
    mine = pltpu.roll(new, lax.rem(KZ - z * KD, KZ), 1)
    jumps_out[...] = mine[:, :KD]
    part = pieces(new)
    for k in range(width // KZ):
        bin_at = lax.broadcasted_iota(jnp.int32, (KZ, KZ), 1).astype(F32) + (start + k * KZ)
        mask = (wide < bin_at).astype(BF16)
        fit = jnp.zeros((KZ, KZ), F32)
        for piece in part[::-1]:
            fit += jnp.dot(piece, mask, preferred_element_type=F32)
        here = slice(k * KZ, (k + 1) * KZ)
        resid[:, here] = signal[:, here] - (fit + left)


def over_samples(stats):
    stats = stats + lax.ppermute(stats, "core", [(0, 1), (1, 0)])
    ring = lambda k: [(i, (i + k) % NY) for i in range(NY)]
    return [stats] + [lax.ppermute(stats, "y", ring(k)) for k in range(1, NY)]


def body(signal, jumps, breaks):
    rows, width = signal.shape
    bins = float(width * NX * NZ)
    (mine,) = call(local_sums, [(2 * KD + 8, rows)], 3, smem=1)(breaks, signal, jumps)
    near = lax.all_to_all(jnp.broadcast_to(mine[None], (NZ,) + mine.shape), "z", 0, 0, tiled=False)
    (group,) = call(functools.partial(group_sums, bins), [(2 * KZ + 8, rows)], 1)(near)
    ring = lambda k: [(i, (i + k) % NX) for i in range(NX)]
    groups = [group] + [lax.ppermute(group, "x", ring(k)) for k in (1, 2, 3)]
    corr, stats = call(first_corr, [(NX, rows, KZ), (16, KZ)], 4)(*groups)
    parts = over_samples(stats)
    jumps1, corr, stats = call(second_corr, [(NX, rows, KZ), (NX, rows, KZ), (16, KZ)], 9)(*groups, corr, *parts)
    parts = over_samples(stats)
    resid, jumps2 = call(functools.partial(finish, bins), [(rows, width), (rows, KD)], 8)(signal, group, jumps1, corr, *parts)
    return resid, jumps2


def solution(mesh):
    fine = Mesh(mesh.devices.reshape(NX, NZ, NY, NC), ("x", "z", "y", "core"))
    both = P(("y", "core"), ("x", "z"))
    return jax.shard_map(
        body,
        mesh=fine,
        in_specs=(both, both, P(("x", "z"))),
        out_specs=(both, both),
        check_vma=False,
    )
```

time: 811 us -> 84.7 us (0.10)
  waiting for transfers between devices: 402 us -> 34.1 us
  blocking collectives: 361 us -> 26.2 us
  between operations: 17.9 us -> 0.7 us
  starting transfers between devices: 0.2 us -> 12.3 us
  other arithmetic: 10.9 us -> 0.01 us
  matrix products: 8.4 us -> 0 us
  Pallas kernels: 0 us -> 8.31 us
    all_gather x5 -> x0, waiting for transfers between devices: 401 us -> none  [steps_of(): shard_part = lax.all_gather(amounts, 'bins', axis=1, tiled=True)]
    psum x6 -> x0, blocking collectives: 299 us -> none  [the longest x2 158 us: body(): grad_sum = lax.psum(jnp.sum(corr * corr), ('bins', 'samp'))]
    all_gather x2 -> x0, blocking collectives: 61.7 us -> none  [entering(): pieces = lax.all_gather(value, axis)]
    ppermute x0 -> x11, waiting for transfers between devices: none -> 34.1 us  [the longest x3 25.8 us: body(): groups = [group] + [lax.ppermute(group, 'x', ring(k)) for k in (1, 2, 3)]]
    all_to_all x0 -> x1, blocking collectives: none -> 26.2 us  [body(): lax.all_to_all(jnp.broadcast_to(mine[None], (NZ,) + mine.shape), 'z', 0,...]
    ppermute x0 -> x11, starting transfers between devices: none -> 12.3 us  [the longest x6 6.01 us: over_samples(): return [stats] + [lax.ppermute(stats, 'y', ring(k)) for k in range(1, NY)]]
    reduce_sum x9 -> x0, other arithmetic: 8.71 us -> none  [the longest x5 7.2 us: steps_of(): left_carry = empty + jnp.sum(jnp.where(before, shard_part, 0.0), axis=1)]
    dot_general x7 -> x0, matrix products: 8.4 us -> none  [the longest x5 4.88 us: steps_of(): inside = jnp.dot(amounts, below_mask, precision=lax.Precision.HIGHEST)]
  transfers between devices with their start and end apart: 5 -> 11, of which waited for: 5 -> 10; matrix products, arithmetic and copies ran while one was open for 0% -> 0% of each run, Pallas kernels for 0% -> 0%
where the time goes in v1:
time: 84.7 us; the launch traced here: 84.5 us
  waiting for transfers between devices  34.1 us (40%)
  blocking collectives  26.2 us (31%)
  starting transfers between devices  12.3 us (15%)
  Pallas kernels  8.31 us (10%)
  local copies, waits for them, and re-layouts  2.82 us (3%)
    all_to_all x1, blocking collectives, body(): lax.all_to_all(jnp.broadcast_to(mine[None], (NZ,) + mine.shape), 'z', 0,...  26.2 us
    ppermute x3, waiting for transfers between devices, body(): groups = [group] + [lax.ppermute(group, 'x', ring(k)) for k in (1, 2, 3)]  25.8 us
    ppermute x6, waiting for transfers between devices, over_samples(): return [stats] + [lax.ppermute(stats, 'y', ring(k)) for k in range(1, NY)]  6.56 us
    ppermute x6, starting transfers between devices, over_samples(): return [stats] + [lax.ppermute(stats, 'y', ring(k)) for k in range(1, NY)]  6.01 us
    ppermute x3, starting transfers between devices, body(): groups = [group] + [lax.ppermute(group, 'x', ring(k)) for k in (1, 2, 3)]  3.67 us
    pallas_call x1, Pallas kernels, body(): call(second_corr, [(NX, rows, KZ), (NX, rows, KZ), (16, KZ)], 9)  2.93 us
    ppermute x2, starting transfers between devices, over_samples(): stats = stats + lax.ppermute(stats, 'core', [(0, 1), (1, 0)])  2.62 us
    unnamed x7, local copies, waits for them, and re-layouts  2.09 us
  transfers between devices with their start and end apart: 11, of which 10 were waited for; matrix products, arithmetic and copies ran while one was open for 0% of the time, Pallas kernels for 0%

profile of v1, /device:TPU:1, one launch (start us, length us, event | category | flops | bytes accessed | tf_op | source)
XLA Modules:
  0.0 84.5 jit_solution(12250544947507711359)
XLA Ops:
  0.6 0.9 %copy.5.jumps = f32[256,32]{1,0:T(8,128)S(1)} copy(f32[256,32]{0,1:T(8,128)} %param.4) | data formatting | bytes 65536 | tf_op args[1]
  1.5 1.2 %copy-done = f32[256,1024]{1,0:T(8,128)S(1)} copy-done((f32[256,1024]{1,0:T(8,128)S(1)}, f32[256,1024]{1,0:T(8,128)}, u32[]{:S(2)}) %copy-start) | copy-done | bytes 1048600
  2.7 1.2 %shard_map.50 = f32[72,256]{1,0:T(8,128)S(1)} custom-call(s32[32]{0:T(128)S(1)} %copy-done.2, f32[256,1024]{1,0:T(8,128)S(1)} %copy-done, f32[256,32]{1,0:T(8,128)S(1)} %copy.5.jumps), custom_call_target="tpu_custom_call" | custom-call | tf_op jit(solution)/shard_map/pallas_call | solution.py:225
  4.0 26.2 %all_to_all.5.got = f32[8,72,256]{2,1,0:T(8,128)S(1)} all-to-all(f32[8,72,256]{2,1,0:T(8,128)S(1)} %broadcast_in_dim.2), channel_id=1, replica_groups=mesh['x'=4,'z'=8,'y'=4,'core'=2] {'z'}, dimensions={0} | all-to-all | bytes 1179648 | tf_op jit(solution)/shard_map/all_to_all | solution.py:226
  30.7 2.6 %collective-permute-start.2 = (f32[520,256]{1,0:T(8,128)S(1)}, f32[520,256]{1,0:T(8,128)S(1)}, u32[]{:S(2)}, u32[]{:S(2)}) collective-permute-start(f32[520,256]{1,0:T(8,128)S(1)} %shard_map.51.g0), channel_id=1, source_target_pairs={{0,192},{64,0},{128,64},{192,128},{1,193},{65,1},{129,65},{193,129... | collective-permute-start | bytes 1597448 | tf_op jit(solution)/shard_map/ppermute | solution.py:229
  33.8 0.6 collective-permute-start
  34.4 8.7 %collective-permute-done.2.g3 = f32[520,256]{1,0:T(8,128)S(1)} collective-permute-done((f32[520,256]{1,0:T(8,128)S(1)}, f32[520,256]{1,0:T(8,128)S(1)}, u32[]{:S(2)}, u32[]{:S(2)}) %collective-permute-start.2) | collective-permute-done | bytes 532512 | tf_op jit(solution)/shard_map/ppermute | solution.py:229
  43.1 2.7 %collective-permute-done.1.g2 = f32[520,256]{1,0:T(8,128)S(1)} collective-permute-done((f32[520,256]{1,0:T(8,128)S(1)}, f32[520,256]{1,0:T(8,128)S(1)}, u32[]{:S(2)}, u32[]{:S(2)}) %collective-permute-start.1) | collective-permute-done | bytes 532512 | tf_op jit(solution)/shard_map/ppermute | solution.py:229
  45.8 14.4 %collective-permute-done.g1 = f32[520,256]{1,0:T(8,128)S(1)} collective-permute-done((f32[520,256]{1,0:T(8,128)S(1)}, f32[520,256]{1,0:T(8,128)S(1)}, u32[]{:S(2)}, u32[]{:S(2)}) %collective-permute-start) | collective-permute-done | bytes 532512 | tf_op jit(solution)/shard_map/ppermute | solution.py:229
  60.2 1.8 %shard_map.52 = (f32[4,256,256]{2,1,0:T(8,128)S(1)}, f32[16,256]{1,0:T(8,128)S(1)}) custom-call(f32[520,256]{1,0:T(8,128)S(1)} %shard_map.51.g0, f32[520,256]{1,0:T(8,128)S(1)} %collective-permute-done.g1, f32[520,256]{1,0:T(8,128)S(1)} %collective-permute-done.1.g2, f32[520,256]{1,0:T(8,128)S(1)} %collective-permute-done.2.g3), custom_call_target="tpu_custom_call" | custom-call | tf_op jit(solution)/shard_map/pallas_call | solution.py:230
  62.0 0.6 collective-permute-start.3
  62.6 0.8 collective-permute-done.3
  63.4 2.7 %collective-permute-start.6 = (f32[16,256]{1,0:T(8,128)S(1)}, f32[16,256]{1,0:T(8,128)S(1)}, u32[]{:S(2)}, u32[]{:S(2)}) collective-permute-start(f32[16,256]{1,0:T(8,128)S(1)} %add.6.s0), channel_id=1, source_target_pairs={{0,6},{2,0},{4,2},{6,4},{1,7},{3,1},{5,3},{7,5},{8,14},{10,8},{12,... | collective-permute-start | bytes 49160 | tf_op jit(solution)/shard_map/ppermute | solution.py:219
  66.5 0.7 collective-permute-start.4
  67.2 3.1 %collective-permute-done.5.s2 = f32[16,256]{1,0:T(8,128)S(1)} collective-permute-done((f32[16,256]{1,0:T(8,128)S(1)}, f32[16,256]{1,0:T(8,128)S(1)}, u32[]{:S(2)}, u32[]{:S(2)}) %collective-permute-start.5) | collective-permute-done | bytes 16416 | tf_op jit(solution)/shard_map/ppermute | solution.py:219
  70.4 2.9 %shard_map.53 = (f32[4,256,256]{2,1,0:T(8,128)S(1)}, f32[4,256,256]{2,1,0:T(8,128)S(1)}, f32[16,256]{1,0:T(8,128)S(1)}) custom-call(f32[520,256]{1,0:T(8,128)S(1)} %shard_map.51.g0, f32[520,256]{1,0:T(8,128)S(1)} %collective-permute-done.g1, f32[520,256]{1,0:T(8,128)S(1)} %collective-permute-done.1.g2, f32[520,256]{1,0:T(8,128)S(1)} %collective-permute-done.2.g3, ...), custom_call_target="tpu_custom_call" | custom-call | tf_op jit(solution)/shard_map/pallas_call | solution.py:232
  73.4 2.0 %collective-permute-start.7 = (f32[16,256]{1,0:T(8,128)S(1)}, f32[16,256]{1,0:T(8,128)S(1)}, u32[]{:S(2)}, u32[]{:S(2)}) collective-permute-start(f32[16,256]{1,0:T(8,128)S(1)} %get-tuple-element.11), channel_id=1, source_target_pairs={{0,1},{1,0},{2,3},{3,2},{4,5},{5,4},{6,7},{7,6},{8,9},{9,8},{10,11... | collective-permute-start | bytes 49160 | tf_op jit(solution)/shard_map/ppermute | solution.py:217
  75.4 0.8 collective-permute-done.7
  76.4 1.3 %collective-permute-start.9 = (f32[16,256]{1,0:T(8,128)S(1)}, f32[16,256]{1,0:T(8,128)S(1)}, u32[]{:S(2)}, u32[]{:S(2)}) collective-permute-start(f32[16,256]{1,0:T(8,128)S(1)} %add.7.s0), channel_id=1, source_target_pairs={{0,4},{2,6},{4,0},{6,2},{1,5},{3,7},{5,1},{7,3},{8,12},{10,14},{12... | collective-permute-start | bytes 49160 | tf_op jit(solution)/shard_map/ppermute | solution.py:219
  77.7 0.8 collective-permute-start.8
  78.8 1.6 %collective-permute-done.9.s2 = f32[16,256]{1,0:T(8,128)S(1)} collective-permute-done((f32[16,256]{1,0:T(8,128)S(1)}, f32[16,256]{1,0:T(8,128)S(1)}, u32[]{:S(2)}, u32[]{:S(2)}) %collective-permute-start.9) | collective-permute-done | bytes 16416 | tf_op jit(solution)/shard_map/ppermute | solution.py:219
  80.4 1.4 %collective-permute-done.8.s1 = f32[16,256]{1,0:T(8,128)S(1)} collective-permute-done((f32[16,256]{1,0:T(8,128)S(1)}, f32[16,256]{1,0:T(8,128)S(1)}, u32[]{:S(2)}, u32[]{:S(2)}) %collective-permute-start.8) | collective-permute-done | bytes 16416 | tf_op jit(solution)/shard_map/ppermute | solution.py:219
  81.8 1.9 %shard_map.54 = (f32[256,1024]{1,0:T(8,128)}, f32[256,32]{1,0:T(8,128)S(1)}) custom-call(f32[256,1024]{1,0:T(8,128)S(1)} %copy-done.1, f32[520,256]{1,0:T(8,128)S(1)} %shard_map.51.g0, f32[4,256,256]{2,1,0:T(8,128)S(1)} %get-tuple-element.9.jumps_in, f32[4,256,256]{2,1,0:T(8,128)S(1)} %get-tuple-element.10.corr_in, f32[16,256]{1,0:T(8,128)S(1)} %add.7.s0, ...), custom_call_target="tpu_custom_call" | custom-call | tf_op jit(solution)/shard_map/pallas_call | solution.py:234
  83.8 0.7 copy.6
  (15 shorter events, 2.0 us)
Async XLA Ops:
  0.6 0.9 %copy-start.2 = (s32[32]{0:T(128)S(1)}, s32[32]{0:T(128)}, u32[]{:S(2)}) copy-start(s32[32]{0:T(128)} %breaks.1) | copy-start | bytes 388
  1.5 1.2 %copy-start = (f32[256,1024]{1,0:T(8,128)S(1)}, f32[256,1024]{1,0:T(8,128)}, u32[]{:S(2)}) copy-start(f32[256,1024]{1,0:T(8,128)} %signal.3) | copy-start | bytes 3145732
  30.7 12.4 %collective-permute-start.2 = (f32[520,256]{1,0:T(8,128)S(1)}, f32[520,256]{1,0:T(8,128)S(1)}, u32[]{:S(2)}, u32[]{:S(2)}) collective-permute-start(f32[520,256]{1,0:T(8,128)S(1)} %shard_map.51.g0), channel_id=1, source_target_pairs={{0,192},{64,0},{128,64},{192,128},{1,193},{65,1},{129,65},{193,129... | collective-permute-start | bytes 1597448 | tf_op jit(solution)/shard_map/ppermute | solution.py:229
  33.3 12.5 %collective-permute-start.1 = (f32[520,256]{1,0:T(8,128)S(1)}, f32[520,256]{1,0:T(8,128)S(1)}, u32[]{:S(2)}, u32[]{:S(2)}) collective-permute-start(f32[520,256]{1,0:T(8,128)S(1)} %shard_map.51.g0), channel_id=1, source_target_pairs={{0,128},{64,192},{128,0},{192,64},{1,129},{65,193},{129,1},{193,65... | collective-permute-start | bytes 1597448 | tf_op jit(solution)/shard_map/ppermute | solution.py:229
  33.8 26.4 %collective-permute-start = (f32[520,256]{1,0:T(8,128)S(1)}, f32[520,256]{1,0:T(8,128)S(1)}, u32[]{:S(2)}, u32[]{:S(2)}) collective-permute-start(f32[520,256]{1,0:T(8,128)S(1)} %shard_map.51.g0), channel_id=1, source_target_pairs={{0,64},{64,128},{128,192},{192,0},{1,65},{65,129},{129,193},{193,1... | collective-permute-start | bytes 1597448 | tf_op jit(solution)/shard_map/ppermute | solution.py:229
  62.0 1.4 %collective-permute-start.3 = (f32[16,256]{1,0:T(8,128)S(1)}, f32[16,256]{1,0:T(8,128)S(1)}, u32[]{:S(2)}, u32[]{:S(2)}) collective-permute-start(f32[16,256]{1,0:T(8,128)S(1)} %get-tuple-element.8), channel_id=1, source_target_pairs={{0,1},{1,0},{2,3},{3,2},{4,5},{5,4},{6,7},{7,6},{8,9},{9,8},{10,11... | collective-permute-start | bytes 49160 | tf_op jit(solution)/shard_map/ppermute | solution.py:217
  63.4 3.8 %collective-permute-start.6 = (f32[16,256]{1,0:T(8,128)S(1)}, f32[16,256]{1,0:T(8,128)S(1)}, u32[]{:S(2)}, u32[]{:S(2)}) collective-permute-start(f32[16,256]{1,0:T(8,128)S(1)} %add.6.s0), channel_id=1, source_target_pairs={{0,6},{2,0},{4,2},{6,4},{1,7},{3,1},{5,3},{7,5},{8,14},{10,8},{12,... | collective-permute-start | bytes 49160 | tf_op jit(solution)/shard_map/ppermute | solution.py:219
  66.1 4.1 %collective-permute-start.5 = (f32[16,256]{1,0:T(8,128)S(1)}, f32[16,256]{1,0:T(8,128)S(1)}, u32[]{:S(2)}, u32[]{:S(2)}) collective-permute-start(f32[16,256]{1,0:T(8,128)S(1)} %add.6.s0), channel_id=1, source_target_pairs={{0,4},{2,6},{4,0},{6,2},{1,5},{3,7},{5,1},{7,3},{8,12},{10,14},{12... | collective-permute-start | bytes 49160 | tf_op jit(solution)/shard_map/ppermute | solution.py:219
  66.5 3.9 %collective-permute-start.4 = (f32[16,256]{1,0:T(8,128)S(1)}, f32[16,256]{1,0:T(8,128)S(1)}, u32[]{:S(2)}, u32[]{:S(2)}) collective-permute-start(f32[16,256]{1,0:T(8,128)S(1)} %add.6.s0), channel_id=1, source_target_pairs={{0,2},{2,4},{4,6},{6,0},{1,3},{3,5},{5,7},{7,1},{8,10},{10,12},{12... | collective-permute-start | bytes 49160 | tf_op jit(solution)/shard_map/ppermute | solution.py:219
  70.4 11.4 %copy-start.1 = (f32[256,1024]{1,0:T(8,128)S(1)}, f32[256,1024]{1,0:T(8,128)}, u32[]{:S(2)}) copy-start(f32[256,1024]{1,0:T(8,128)} %signal.3) | copy-start | bytes 3145732
  73.4 2.9 %collective-permute-start.7 = (f32[16,256]{1,0:T(8,128)S(1)}, f32[16,256]{1,0:T(8,128)S(1)}, u32[]{:S(2)}, u32[]{:S(2)}) collective-permute-start(f32[16,256]{1,0:T(8,128)S(1)} %get-tuple-element.11), channel_id=1, source_target_pairs={{0,1},{1,0},{2,3},{3,2},{4,5},{5,4},{6,7},{7,6},{8,9},{9,8},{10,11... | collective-permute-start | bytes 49160 | tf_op jit(solution)/shard_map/ppermute | solution.py:217
  76.2 2.6 %collective-permute-start.10 = (f32[16,256]{1,0:T(8,128)S(1)}, f32[16,256]{1,0:T(8,128)S(1)}, u32[]{:S(2)}, u32[]{:S(2)}) collective-permute-start(f32[16,256]{1,0:T(8,128)S(1)} %add.7.s0), channel_id=1, source_target_pairs={{0,6},{2,0},{4,2},{6,4},{1,7},{3,1},{5,3},{7,5},{8,14},{10,8},{12,... | collective-permute-start | bytes 49160 | tf_op jit(solution)/shard_map/ppermute | solution.py:219
  76.4 4.1 %collective-permute-start.9 = (f32[16,256]{1,0:T(8,128)S(1)}, f32[16,256]{1,0:T(8,128)S(1)}, u32[]{:S(2)}, u32[]{:S(2)}) collective-permute-start(f32[16,256]{1,0:T(8,128)S(1)} %add.7.s0), channel_id=1, source_target_pairs={{0,4},{2,6},{4,0},{6,2},{1,5},{3,7},{5,1},{7,3},{8,12},{10,14},{12... | collective-permute-start | bytes 49160 | tf_op jit(solution)/shard_map/ppermute | solution.py:219
  77.7 4.1 %collective-permute-start.8 = (f32[16,256]{1,0:T(8,128)S(1)}, f32[16,256]{1,0:T(8,128)S(1)}, u32[]{:S(2)}, u32[]{:S(2)}) collective-permute-start(f32[16,256]{1,0:T(8,128)S(1)} %add.7.s0), channel_id=1, source_target_pairs={{0,2},{2,4},{4,6},{6,0},{1,3},{3,5},{5,7},{7,1},{8,10},{10,12},{12... | collective-permute-start | bytes 49160 | tf_op jit(solution)/shard_map/ppermute | solution.py:219

commit v2 on v1

v2 whole, which is shorter than its diff:
```python
import functools

import jax
import jax.numpy as jnp
from jax import lax
from jax.experimental import pallas as pl
from jax.experimental.pallas import tpu as pltpu
from jax.sharding import Mesh, PartitionSpec as P

EPS = 1e-06
SHRINK = 0.5
NX, NZ, NY, NC = 4, 8, 4, 2
KD = 32
KZ = KD * NZ
F32 = jnp.float32
BF16 = jnp.bfloat16
VMEM = pl.BlockSpec(memory_space=pltpu.VMEM)
SMEM = pl.BlockSpec(memory_space=pltpu.SMEM)
HBM = pl.BlockSpec(memory_space=pltpu.HBM)
CHUNK = 256


def pieces(v):
    hi = v.astype(BF16)
    rest = v - hi.astype(F32)
    mid = rest.astype(BF16)
    low = (rest - mid.astype(F32)).astype(BF16)
    return hi, mid, low


def mul(a, b):
    return jnp.dot(a, b, preferred_element_type=F32)


def times_overlap(v, overlap):
    high, low = overlap
    a, b, _ = pieces(v)
    return (mul(b, high) + mul(a, low)) + mul(a, high)


def call(kernel, out_shape, in_specs, out_specs=None, scratch=()):
    return pl.pallas_call(
        kernel,
        out_shape=[jax.ShapeDtypeStruct(s, F32) for s in out_shape],
        in_specs=in_specs,
        out_specs=out_specs or [VMEM] * len(out_shape),
        scratch_shapes=list(scratch),
        compiler_params=pltpu.CompilerParams(vmem_limit_bytes=32 << 20),
    )


def local_sums(breaks, signal, jumps, out, at_smem, held, sems, sem2):
    rows, width = signal.shape
    marks_in = pltpu.make_async_copy(breaks, at_smem, sem2.at[0])
    marks_in.start()
    parts = [slice(k, k + CHUNK) for k in range(0, width, CHUNK)]
    copies = [pltpu.make_async_copy(signal.at[:, part], held.at[:, part], sems.at[i]) for i, part in enumerate(parts)]
    for copy in copies:
        copy.start()
    jumps_in = pltpu.make_async_copy(jumps, out.at[0:KD, :], sem2.at[1])
    jumps_in.start()
    z = lax.axis_index("z")
    start = (lax.axis_index("x") * NZ + z) * width
    sub = lax.broadcasted_iota(jnp.int32, (40, 128), 0)
    lane = lax.broadcasted_iota(jnp.int32, (8, KZ), 1)
    at = jnp.where(sub == KD, -1, width)
    row = jnp.zeros((8, KZ), jnp.int32)
    marks_in.wait()
    for k in range(KD):
        mark = at_smem[k]
        at = jnp.where(sub == k, mark - start, at)
        row = jnp.where(lane == z * KD + k, mark, row)
    at = jnp.concatenate([at] * (CHUNK // 128), axis=1)
    bin_at = lax.broadcasted_iota(jnp.int32, (40, CHUNK), 1)
    total = jnp.zeros((40, rows), F32)
    for copy, part in zip(copies, parts):
        mask = (bin_at + part.start > at).astype(BF16)
        copy.wait()
        for piece in pieces(held[:, part])[::-1]:
            total += lax.dot_general(mask, piece, (((1,), (1,)), ((), ())), preferred_element_type=F32)
    out[KD : 2 * KD, :] = total[:KD]
    sub8 = lax.broadcasted_iota(jnp.int32, (8, KZ), 0)
    out[2 * KD :, :] = jnp.where(sub8 == 1, row.astype(F32), total[KD:])
    jumps_in.wait()


def gram(after):
    wide = jnp.broadcast_to(after, (KZ, KZ))
    both = jnp.minimum(wide, wide.T)
    high = both.astype(BF16)
    return high, (both - high.astype(F32)).astype(BF16)


def column_sum(v):
    return jnp.sum(v, axis=0, keepdims=True)


TOTAL, JUMPS, WEIGHTED, AFTER, CORR = range(5)


def group_sums(bins, got, big, small):
    head = got[...]
    after = (bins - 1.0) - column_sum(head[:, 2 * KD + 1, :])
    wide = jnp.broadcast_to(after, (KZ, KZ)).T
    overlap = jnp.minimum(jnp.broadcast_to(after, (KZ, KZ)), wide)
    jumps = head[:, :KD, :].reshape(KZ, KZ)
    later = jnp.zeros((1, KZ), F32)
    behind = [None] * NZ
    for z in range(NZ - 1, -1, -1):
        behind[z] = head[z, KD : 2 * KD, :] + later
        later = later + head[z, 2 * KD : 2 * KD + 1, :]
    own = jnp.dot(overlap, jumps, precision=lax.Precision.HIGHEST, preferred_element_type=F32)
    corr = jnp.concatenate(behind, axis=0) - own
    small[TOTAL : TOTAL + 1, :] = later
    small[JUMPS : JUMPS + 1, :] = column_sum(jumps)
    small[WEIGHTED : WEIGHTED + 1, :] = column_sum(jumps * wide)
    small[AFTER : AFTER + 1, :] = after
    small[CORR : CORR + 1, :] = column_sum(corr)
    small[CORR + 1 :, :] = jnp.zeros((7 - CORR, KZ), F32)
    big[0:KZ, :] = jumps.T
    big[KZ:, :] = corr.T


def places():
    x = lax.axis_index("x")
    return [lax.rem(x + NX - k, NX) for k in range(NX)]


def weights(place):
    one = lambda c: jnp.where(c, 1.0, 0.0).astype(F32)
    return [[one(place[q] < place[p]) for q in range(NX)] for p in range(NX)]


def weigh(before, p, values, later=False):
    out = 0.0
    for q in range(NX):
        if q != p:
            out = out + (before[q][p] if later else before[p][q]) * values[q]
    return out


def base_rows(before, smalls):
    row = lambda p, k: smalls[p][k : k + 1, :]
    lower = [weigh(before, p, [row(q, JUMPS) for q in range(NX)]) for p in range(NX)]
    upper = [weigh(before, p, [row(q, TOTAL) - row(q, WEIGHTED) for q in range(NX)], True) for p in range(NX)]
    return lower, upper


def own_stats(big, ms, stats):
    place = places()
    smalls = [ms.at[k] for k in place]
    m0 = smalls[0]
    before = weights(place)
    lower, upper = base_rows(before, smalls)
    after = m0[AFTER : AFTER + 1, :]
    columns = jnp.concatenate([lower[0], upper[0]] + [jnp.zeros((6, KZ), F32)], axis=0).T
    jumps = big[0:KZ, :]
    corr = big[KZ:, :] + columns[:, 1:2] - columns[:, 0:1] * after
    sums = []
    for p in range(NX):
        reach = jnp.sum(smalls[p][AFTER : AFTER + 1, :], axis=1, keepdims=True)
        sums.append(smalls[p][CORR : CORR + 1, :] + float(KZ) * upper[p] - reach * lower[p])
    lead = weigh(before, 0, sums)
    weighted = jnp.sum(corr * after, axis=1, keepdims=True)
    cross = 2.0 * jnp.sum(weighted * jnp.broadcast_to(lead, (8, KZ)).T[:, 0:1])
    curv = column_sum(corr * times_overlap(corr, gram(after)))
    lane = lax.broadcasted_iota(jnp.int32, (1, KZ), 1)
    stats[0:1, :] = column_sum(jumps * jumps)
    stats[1:2, :] = column_sum(jumps * corr)
    stats[2:3, :] = column_sum(corr * corr)
    stats[3:4, :] = curv + jnp.where(lane == 0, cross, 0.0)
    stats[4:, :] = jnp.zeros((4, KZ), F32)


def shrink_of(rows):
    grad, curv = rows(0, 2), rows(0, 3)
    for p in range(1, NX):
        grad, curv = grad + rows(p, 2), curv + rows(p, 3)
    step = jnp.sum(grad, axis=1, keepdims=True) / (jnp.sum(curv, axis=1, keepdims=True) + EPS)
    norms, level = [], 0.0
    for p in range(NX):
        square = rows(p, 0) + 2.0 * step * rows(p, 1) + step * step * rows(p, 2)
        norms.append(jnp.sqrt(jnp.maximum(square, 0.0) + EPS))
        level = level + norms[-1]
    level = jnp.sum(level, axis=1, keepdims=True) / (NX * KZ)
    return step, [jnp.maximum(0.0, 1.0 - SHRINK * level / n) for n in norms]


def second_corr(b0, b1, b2, b3, ms, ss, jumps_out, corr_out, stats):
    place = places()
    smalls = [ms.at[k] for k in place]
    bigs, sums_in = (b0, b1, b2, b3), [ss.at[k] for k in place]
    before = weights(place)
    after = [m[AFTER : AFTER + 1, :] for m in smalls]
    overlap = [gram(a) for a in after]
    lower, upper = base_rows(before, smalls)
    columns = jnp.concatenate(lower + upper, axis=0).T
    step, factor = shrink_of(lambda p, k: sums_in[p][k : k + 1, :])
    jumps, corr, change, sums, weighted = [], [], [], [], []
    for p in range(NX):
        j = bigs[p][0:KZ, :]
        c = bigs[p][KZ:, :] + columns[:, NX + p : NX + p + 1] - columns[:, p : p + 1] * after[p]
        new = factor[p] * (j + step * c)
        d = new - j
        jumps_out[p] = new
        jumps.append(new)
        corr.append(c)
        change.append(d)
        sums.append(jnp.sum(d, axis=1, keepdims=True))
        weighted.append(jnp.sum(d * after[p], axis=1, keepdims=True))
    for p in range(NX):
        low, high = weigh(before, p, sums), weigh(before, p, weighted, True)
        corr[p] = corr[p] - times_overlap(change[p], overlap[p]) - low * after[p] - high
        corr_out[p] = corr[p]
    curv = jnp.zeros((1, KZ), F32)
    for p in range(NX):
        c, j = corr[p], jumps[p]
        sums[p] = jnp.sum(c, axis=1, keepdims=True)
        weighted[p] = jnp.sum(c * after[p], axis=1, keepdims=True)
        stats[4 * p : 4 * p + 1, :] = column_sum(j * j)
        stats[4 * p + 1 : 4 * p + 2, :] = column_sum(j * c)
        stats[4 * p + 2 : 4 * p + 3, :] = column_sum(c * c)
        curv += column_sum(c * times_overlap(c, overlap[p]))
    cross = jnp.zeros((KZ, 1), F32)
    for p in range(NX):
        cross += weighted[p] * weigh(before, p, sums)
    lane = lax.broadcasted_iota(jnp.int32, (1, KZ), 1)
    stats[3:4, :] = curv + jnp.where(lane == 0, 2.0 * jnp.sum(cross), 0.0)
    for p in range(1, NX):
        stats[4 * p + 3 : 4 * p + 4, :] = jnp.zeros((1, KZ), F32)


def finish(bins, signal, m0, jumps_in, corr_in, s0, s1, s2, s3, resid, jumps_out, held, sems):
    before = weights(places())[0]
    x, z = lax.axis_index("x"), lax.axis_index("z")
    width = signal.shape[1]
    total = (s0[...] + s1[...]) + (s2[...] + s3[...])
    step, factor = shrink_of(lambda p, k: total[4 * p + k : 4 * p + k + 1, :])
    left = jnp.zeros((KZ, KZ), F32)
    for p in range(1, NX):
        left += (before[p] * factor[p]) * (jumps_in[p] + step * corr_in[p])
    left = jnp.sum(left, axis=1, keepdims=True)
    new = factor[0] * (jumps_in[0] + step * corr_in[0])
    marks = (bins - 1.0) - m0[AFTER : AFTER + 1, :]
    wide = jnp.broadcast_to(marks, (KZ, KZ)).T
    start = ((x * NZ + z) * width).astype(F32)
    part = pieces(new)
    copies = []
    for i in range(width // CHUNK):
        bin_at = lax.broadcasted_iota(jnp.int32, (KZ, CHUNK), 1).astype(F32) + (start + i * CHUNK)
        mask = (wide < bin_at).astype(BF16)
        fit = jnp.zeros((KZ, CHUNK), F32)
        for piece in part[::-1]:
            fit += mul(piece, mask)
        here = slice(i * CHUNK, (i + 1) * CHUNK)
        held[:, here] = signal[:, here] - (fit + left)
        copies.append(pltpu.make_async_copy(held.at[:, here], resid.at[:, here], sems.at[i]))
        copies[-1].start()
    jumps_out[...] = pltpu.roll(new, lax.rem(KZ - z * KD, KZ), 1)[:, :128].T[:KD]
    for copy in copies:
        copy.wait()


def round_x(block):
    ring = lambda k: [(i, (i + k) % NX) for i in range(NX)]
    return [block] + [lax.ppermute(block, "x", ring(k)) for k in range(1, NX)]


def over_samples(stats):
    stats = stats + lax.ppermute(stats, "core", [(0, 1), (1, 0)])
    ring = lambda k: [(i, (i + k) % NY) for i in range(NY)]
    return [stats] + [lax.ppermute(stats, "y", ring(k)) for k in range(1, NY)]


def body(signal, jumps, breaks):
    rows, width = signal.shape
    bins = float(width * NX * NZ)
    slab = [pltpu.VMEM((rows, width), F32), pltpu.SemaphoreType.DMA((width // CHUNK,))]
    first = call(
        local_sums,
        [(2 * KD + 8, rows)],
        [HBM] * 3,
        scratch=[pltpu.SMEM((KD,), jnp.int32)] + slab + [pltpu.SemaphoreType.DMA((2,))],
    )
    (mine,) = first(*[pltpu.with_memory_space_constraint(a, pltpu.HBM) for a in (breaks, signal, jumps.T)])
    near = lax.all_to_all(jnp.broadcast_to(mine[None], (NZ,) + mine.shape), "z", 0, 0, tiled=False)
    big, small = call(functools.partial(group_sums, bins), [(2 * KZ, rows), (8, rows)], [VMEM])(near)
    ring = lambda k: [(i, (i + k) % NX) for i in range(NX)]
    b1, b3 = lax.ppermute(big, "x", ring(1)), lax.ppermute(big, "x", ring(3))
    smalls = lax.all_to_all(jnp.broadcast_to(small[None], (NX,) + small.shape), "x", 0, 0, tiled=False)
    bg, smalls = lax.optimization_barrier((big, smalls))
    bigs = [big, b1, lax.ppermute(bg, "x", ring(2)), b3]
    (stats,) = call(own_stats, [(8, KZ)], [VMEM] * 2)(big, smalls)
    stats = stats + lax.ppermute(stats, "core", [(0, 1), (1, 0)])
    stats = lax.all_to_all(jnp.broadcast_to(stats[None], (NY,) + stats.shape), "y", 0, 0, tiled=False).sum(0)
    sums = lax.all_to_all(jnp.broadcast_to(stats[None], (NX,) + stats.shape), "x", 0, 0, tiled=False)
    jumps1, corr, stats = call(second_corr, [(NX, rows, KZ), (NX, rows, KZ), (16, KZ)], [VMEM] * 6)(*bigs, smalls, sums)
    parts = over_samples(stats)
    last = call(functools.partial(finish, bins), [(rows, width), (KD, rows)], [VMEM] * 8, [HBM, VMEM], slab)
    resid, jumps2 = last(signal, small, jumps1, corr, *parts)
    return resid, jumps2.T


def solution(mesh):
    fine = Mesh(mesh.devices.reshape(NX, NZ, NY, NC), ("x", "z", "y", "core"))
    both = P(("y", "core"), ("x", "z"))
    return jax.shard_map(
        body,
        mesh=fine,
        in_specs=(both, both, P(("x", "z"))),
        out_specs=(both, both),
        check_vma=False,
    )
```

time: 84.7 us -> 77.1 us (0.910)
  waiting for transfers between devices: 34.1 us -> 6.52 us
  blocking collectives: 26.2 us -> 44.1 us
  starting transfers between devices: 12.3 us -> 17 us
  local copies, waits for them, and re-layouts: 2.82 us -> 0.68 us
    ppermute x3 -> x4, waiting for transfers between devices: 25.8 us -> 0.84 us  [the longest x1 0.83 us: body(): stats = stats + lax.ppermute(stats, 'core', [(0, 1), (1, 0)])]
    all_to_all x0 -> x2, blocking collectives: none -> 17.8 us  [the longest x1 9.55 us: body(): lax.all_to_all(jnp.broadcast_to(stats[None], (NX,) + stats.shape), 'x', 0...]
    ppermute x3 -> x4, starting transfers between devices: 3.67 us -> 7.84 us  [the longest x1 4.36 us: body(): stats = stats + lax.ppermute(stats, 'core', [(0, 1), (1, 0)])]
    all_to_all x0 -> x1, starting transfers between devices: none -> 4.01 us  [body(): lax.all_to_all(jnp.broadcast_to(small[None], (NX,) + small.shape), 'x', 0...]
    ppermute x6 -> x3, waiting for transfers between devices: 6.56 us -> 3.23 us  [over_samples(): return [stats] + [lax.ppermute(stats, 'y', ring(k)) for k in range(1, NY)]]
    ppermute x6 -> x3, starting transfers between devices: 6.01 us -> 3.73 us  [over_samples(): return [stats] + [lax.ppermute(stats, 'y', ring(k)) for k in range(1, NY)]]
    unnamed x7 -> x2, local copies, waits for them, and re-layouts: 2.09 us -> 0.01 us
    all_to_all x0 -> x1, waiting for transfers between devices: none -> 1.62 us  [body(): lax.all_to_all(jnp.broadcast_to(small[None], (NX,) + small.shape), 'x', 0...]
  transfers between devices with their start and end apart: 11 -> 9, of which waited for: 10 -> 5; matrix products, arithmetic and copies ran while one was open for 0% -> 0% of each run, Pallas kernels for 0% -> 1%
where the time goes in v2:
time: 77.1 us; the launch traced here: 76.8 us
  blocking collectives  44.1 us (57%)
  starting transfers between devices  17 us (22%)
  Pallas kernels  7.91 us (10%)
  waiting for transfers between devices  6.52 us (8%)
    all_to_all x1, blocking collectives, body(): lax.all_to_all(jnp.broadcast_to(mine[None], (NZ,) + mine.shape), 'z', 0,...  26.2 us
    all_to_all x1, blocking collectives, body(): lax.all_to_all(jnp.broadcast_to(stats[None], (NX,) + stats.shape), 'x', 0...  9.55 us
    all_to_all x1, blocking collectives, body(): lax.all_to_all(jnp.broadcast_to(stats[None], (NY,) + stats.shape), 'y', 0...  8.27 us
    ppermute x1, starting transfers between devices, body(): stats = stats + lax.ppermute(stats, 'core', [(0, 1), (1, 0)])  4.36 us
    all_to_all x1, starting transfers between devices, body(): lax.all_to_all(jnp.broadcast_to(small[None], (NX,) + small.shape), 'x', 0...  4.01 us
    ppermute x3, starting transfers between devices, over_samples(): return [stats] + [lax.ppermute(stats, 'y', ring(k)) for k in range(1, NY)]  3.73 us
    ppermute x3, waiting for transfers between devices, over_samples(): return [stats] + [lax.ppermute(stats, 'y', ring(k)) for k in range(1, NY)]  3.23 us
    ppermute x2, starting transfers between devices, body(): b1, b3 = (lax.ppermute(big, 'x', ring(1)), lax.ppermute(big, 'x', ring(3)))  2.68 us
  transfers between devices with their start and end apart: 9, of which 5 were waited for; matrix products, arithmetic and copies ran while one was open for 0% of the time, Pallas kernels for 1%

profile of v2, /device:TPU:1, one launch (start us, length us, event | category | flops | bytes accessed | tf_op | source)
XLA Modules:
  0.0 76.8 jit_solution(15337716621570291277)
XLA Ops:
  0.6 2.1 %shard_map.50 = f32[72,256]{1,0:T(8,128)S(1)} custom-call(s32[32]{0:T(128)} %breaks.1, f32[256,1024]{1,0:T(8,128)} %signal.3, f32[32,256]{1,0:T(8,128)} %bitcast.2), custom_call_target="tpu_custom_call" | custom-call | tf_op jit(solution)/shard_map/pallas_call | solution.py:285
  2.8 26.2 %all_to_all.20.got = f32[8,72,256]{2,1,0:T(8,128)S(1)} all-to-all(f32[8,72,256]{2,1,0:T(8,128)S(1)} %broadcast_in_dim.8), channel_id=1, replica_groups=mesh['x'=4,'z'=8,'y'=4,'core'=2] {'z'}, dimensions={0} | all-to-all | bytes 1179648 | tf_op jit(solution)/shard_map/all_to_all | solution.py:286
  29.1 0.5 shard_map.51
  29.6 0.6 broadcast_in_dim.9
  30.2 4.0 %all-to-all-start.1 = ((f32[4,8,256]{2,1,0:T(8,128)}), f32[4,8,256]{2,1,0:T(8,128)S(1)}, u32[]{:S(2)}, u32[]{:S(2)}) async-start(f32[4,8,256]{2,1,0:T(8,128)} %broadcast_in_dim.9), calls=%async_computation.1 | async-start | bytes 65536 | tf_op jit(solution)/shard_map/all_to_all | solution.py:290
  34.2 2.7 %collective-permute-start.2 = (f32[512,256]{1,0:T(8,128)S(1)}, f32[512,256]{1,0:T(8,128)S(1)}, u32[]{:S(2)}, u32[]{:S(2)}) collective-permute-start(f32[512,256]{1,0:T(8,128)S(1)} %get-tuple-element.13.big.b0), channel_id=1, source_target_pairs={{0,192},{64,0},{128,64},{192,128},{1,193},{65,1},{129,65},{193,129... | collective-permute-start | bytes 1572872 | tf_op jit(solution)/shard_map/ppermute | solution.py:289
  36.9 0.0 collective-permute-start
  36.9 1.6 %all-to-all-done.1.ms = f32[4,8,256]{2,1,0:T(8,128)S(1)} async-done(((f32[4,8,256]{2,1,0:T(8,128)}), f32[4,8,256]{2,1,0:T(8,128)S(1)}, u32[]{:S(2)}, u32[]{:S(2)}) %all-to-all-start.1) | async-done | bytes 32800 | tf_op jit(solution)/shard_map/all_to_all | solution.py:290
  38.5 0.8 %collective-permute-start.1 = (f32[512,256]{1,0:T(8,128)S(1)}, f32[512,256]{1,0:T(8,128)S(1)}, u32[]{:S(2)}, u32[]{:S(2)}) collective-permute-start(f32[512,256]{1,0:T(8,128)S(1)} %get-tuple-element.13.big.b0), channel_id=1, source_target_pairs={{0,128},{64,192},{128,0},{192,64},{1,129},{65,193},{129,1},{193,65... | collective-permute-start | bytes 1572872 | tf_op jit(solution)/shard_map/ppermute | solution.py:292
  39.3 0.6 shard_map.52
  39.9 4.4 %collective-permute-start.3 = (f32[8,256]{1,0:T(8,128)S(1)}, f32[8,256]{1,0:T(8,128)S(1)}, u32[]{:S(2)}, u32[]{:S(2)}) collective-permute-start(f32[8,256]{1,0:T(8,128)S(1)} %shard_map.52), channel_id=1, source_target_pairs={{0,1},{1,0},{2,3},{3,2},{4,5},{5,4},{6,7},{7,6},{8,9},{9,8},{10,11... | collective-permute-start | bytes 24584 | tf_op jit(solution)/shard_map/ppermute | solution.py:294
  44.3 0.8 %collective-permute-done.3 = f32[8,256]{1,0:T(8,128)S(1)} collective-permute-done((f32[8,256]{1,0:T(8,128)S(1)}, f32[8,256]{1,0:T(8,128)S(1)}, u32[]{:S(2)}, u32[]{:S(2)}) %collective-permute-start.3) | collective-permute-done | bytes 8224 | tf_op jit(solution)/shard_map/ppermute | solution.py:294
  45.1 8.3 %all_to_all.21 = f32[4,8,256]{2,1,0:T(8,128)S(1)} all-to-all(f32[4,8,256]{2,1,0:T(8,128)S(1)} %broadcast_in_dim.10), channel_id=1, replica_groups=mesh['x'=4,'z'=8,'y'=4,'core'=2] {'y'}, dimensions={0} | all-to-all | bytes 65536 | tf_op jit(solution)/shard_map/all_to_all | solution.py:295
  53.4 9.6 %all_to_all.22.ss = f32[4,8,256]{2,1,0:T(8,128)S(1)} all-to-all(f32[4,8,256]{2,1,0:T(8,128)S(1)} %broadcast_in_dim.11), channel_id=1, replica_groups=mesh['x'=4,'z'=8,'y'=4,'core'=2] {'x'}, dimensions={0} | all-to-all | bytes 65536 | tf_op jit(solution)/shard_map/all_to_all | solution.py:296
  63.0 0.0 collective-permute-done.2.b3
  63.0 2.3 %shard_map.53 = (f32[4,256,256]{2,1,0:T(8,128)S(1)}, f32[4,256,256]{2,1,0:T(8,128)S(1)}, f32[16,256]{1,0:T(8,128)S(1)}) custom-call(f32[512,256]{1,0:T(8,128)S(1)} %get-tuple-element.13.big.b0, f32[512,256]{1,0:T(8,128)S(1)} %collective-permute-done.b1, f32[512,256]{1,0:T(8,128)S(1)} %collective-permute-done.1.b2, f32[512,256]{1,0:T(8,128)S(1)} %collective-permute-done.2.b3, ...), custom_call_target="tpu_custom_call" | custom-call | tf_op jit(solution)/shard_map/pallas_call | solution.py:297
  65.3 1.4 %collective-permute-start.4 = (f32[16,256]{1,0:T(8,128)S(1)}, f32[16,256]{1,0:T(8,128)S(1)}, u32[]{:S(2)}, u32[]{:S(2)}) collective-permute-start(f32[16,256]{1,0:T(8,128)S(1)} %get-tuple-element.17), channel_id=1, source_target_pairs={{0,1},{1,0},{2,3},{3,2},{4,5},{5,4},{6,7},{7,6},{8,9},{9,8},{10,11... | collective-permute-start | bytes 49160 | tf_op jit(solution)/shard_map/ppermute | solution.py:270
  66.7 0.8 %collective-permute-done.4 = f32[16,256]{1,0:T(8,128)S(1)} collective-permute-done((f32[16,256]{1,0:T(8,128)S(1)}, f32[16,256]{1,0:T(8,128)S(1)}, u32[]{:S(2)}, u32[]{:S(2)}) %collective-permute-start.4) | collective-permute-done | bytes 16416 | tf_op jit(solution)/shard_map/ppermute | solution.py:270
  67.5 2.7 %collective-permute-start.7 = (f32[16,256]{1,0:T(8,128)S(1)}, f32[16,256]{1,0:T(8,128)S(1)}, u32[]{:S(2)}, u32[]{:S(2)}) collective-permute-start(f32[16,256]{1,0:T(8,128)S(1)} %add.7.s0), channel_id=1, source_target_pairs={{0,6},{2,0},{4,2},{6,4},{1,7},{3,1},{5,3},{7,5},{8,14},{10,8},{12,... | collective-permute-start | bytes 49160 | tf_op jit(solution)/shard_map/ppermute | solution.py:272
  70.2 0.3 collective-permute-start.6
  70.5 0.7 collective-permute-start.5
  71.2 3.1 %collective-permute-done.6.s2 = f32[16,256]{1,0:T(8,128)S(1)} collective-permute-done((f32[16,256]{1,0:T(8,128)S(1)}, f32[16,256]{1,0:T(8,128)S(1)}, u32[]{:S(2)}, u32[]{:S(2)}) %collective-permute-start.6) | collective-permute-done | bytes 16416 | tf_op jit(solution)/shard_map/ppermute | solution.py:272
  74.3 0.2 collective-permute-done.5.s1
  74.5 2.4 %shard_map.54 = (f32[256,1024]{1,0:T(8,128)}, f32[32,256]{1,0:T(8,128)}) custom-call(f32[256,1024]{1,0:T(8,128)S(1)} %copy-done, f32[8,256]{1,0:T(8,128)S(1)} %get-tuple-element.11.m0, f32[4,256,256]{2,1,0:T(8,128)S(1)} %get-tuple-element.15.jumps_in, f32[4,256,256]{2,1,0:T(8,128)S(1)} %get-tuple-element.16.corr_in, f32[16,256]{1,0:T(8,128)S(1)} %add.7.s0, ...), custom_call_target="tpu_custom_call" | custom-call | tf_op jit(solution)/shard_map/pallas_call | solution.py:300
  (11 shorter events, 0.1 us)
Async XLA Ops:
  30.2 8.3 %all-to-all-start.1 = ((f32[4,8,256]{2,1,0:T(8,128)}), f32[4,8,256]{2,1,0:T(8,128)S(1)}, u32[]{:S(2)}, u32[]{:S(2)}) async-start(f32[4,8,256]{2,1,0:T(8,128)} %broadcast_in_dim.9), calls=%async_computation.1 | async-start | bytes 65536 | tf_op jit(solution)/shard_map/all_to_all | solution.py:290
  34.2 28.8 %collective-permute-start.2 = (f32[512,256]{1,0:T(8,128)S(1)}, f32[512,256]{1,0:T(8,128)S(1)}, u32[]{:S(2)}, u32[]{:S(2)}) collective-permute-start(f32[512,256]{1,0:T(8,128)S(1)} %get-tuple-element.13.big.b0), channel_id=1, source_target_pairs={{0,192},{64,0},{128,64},{192,128},{1,193},{65,1},{129,65},{193,129... | collective-permute-start | bytes 1572872 | tf_op jit(solution)/shard_map/ppermute | solution.py:289
  36.9 26.1 %collective-permute-start = (f32[512,256]{1,0:T(8,128)S(1)}, f32[512,256]{1,0:T(8,128)S(1)}, u32[]{:S(2)}, u32[]{:S(2)}) collective-permute-start(f32[512,256]{1,0:T(8,128)S(1)} %get-tuple-element.13.big.b0), channel_id=1, source_target_pairs={{0,64},{64,128},{128,192},{192,0},{1,65},{65,129},{129,193},{193,1... | collective-permute-start | bytes 1572872 | tf_op jit(solution)/shard_map/ppermute | solution.py:289
  38.5 24.5 %collective-permute-start.1 = (f32[512,256]{1,0:T(8,128)S(1)}, f32[512,256]{1,0:T(8,128)S(1)}, u32[]{:S(2)}, u32[]{:S(2)}) collective-permute-start(f32[512,256]{1,0:T(8,128)S(1)} %get-tuple-element.13.big.b0), channel_id=1, source_target_pairs={{0,128},{64,192},{128,0},{192,64},{1,129},{65,193},{129,1},{193,65... | collective-permute-start | bytes 1572872 | tf_op jit(solution)/shard_map/ppermute | solution.py:292
  39.9 5.2 %collective-permute-start.3 = (f32[8,256]{1,0:T(8,128)S(1)}, f32[8,256]{1,0:T(8,128)S(1)}, u32[]{:S(2)}, u32[]{:S(2)}) collective-permute-start(f32[8,256]{1,0:T(8,128)S(1)} %shard_map.52), channel_id=1, source_target_pairs={{0,1},{1,0},{2,3},{3,2},{4,5},{5,4},{6,7},{7,6},{8,9},{9,8},{10,11... | collective-permute-start | bytes 24584 | tf_op jit(solution)/shard_map/ppermute | solution.py:294
  63.0 11.5 %copy-start = (f32[256,1024]{1,0:T(8,128)S(1)}, f32[256,1024]{1,0:T(8,128)}, u32[]{:S(2)}) copy-start(f32[256,1024]{1,0:T(8,128)} %signal.3) | copy-start | bytes 3145732
  65.3 2.2 %collective-permute-start.4 = (f32[16,256]{1,0:T(8,128)S(1)}, f32[16,256]{1,0:T(8,128)S(1)}, u32[]{:S(2)}, u32[]{:S(2)}) collective-permute-start(f32[16,256]{1,0:T(8,128)S(1)} %get-tuple-element.17), channel_id=1, source_target_pairs={{0,1},{1,0},{2,3},{3,2},{4,5},{5,4},{6,7},{7,6},{8,9},{9,8},{10,11... | collective-permute-start | bytes 49160 | tf_op jit(solution)/shard_map/ppermute | solution.py:270
  67.5 3.7 %collective-permute-start.7 = (f32[16,256]{1,0:T(8,128)S(1)}, f32[16,256]{1,0:T(8,128)S(1)}, u32[]{:S(2)}, u32[]{:S(2)}) collective-permute-start(f32[16,256]{1,0:T(8,128)S(1)} %add.7.s0), channel_id=1, source_target_pairs={{0,6},{2,0},{4,2},{6,4},{1,7},{3,1},{5,3},{7,5},{8,14},{10,8},{12,... | collective-permute-start | bytes 49160 | tf_op jit(solution)/shard_map/ppermute | solution.py:272
  70.2 4.1 %collective-permute-start.6 = (f32[16,256]{1,0:T(8,128)S(1)}, f32[16,256]{1,0:T(8,128)S(1)}, u32[]{:S(2)}, u32[]{:S(2)}) collective-permute-start(f32[16,256]{1,0:T(8,128)S(1)} %add.7.s0), channel_id=1, source_target_pairs={{0,4},{2,6},{4,0},{6,2},{1,5},{3,7},{5,1},{7,3},{8,12},{10,14},{12... | collective-permute-start | bytes 49160 | tf_op jit(solution)/shard_map/ppermute | solution.py:272
  70.5 3.9 %collective-permute-start.5 = (f32[16,256]{1,0:T(8,128)S(1)}, f32[16,256]{1,0:T(8,128)S(1)}, u32[]{:S(2)}, u32[]{:S(2)}) collective-permute-start(f32[16,256]{1,0:T(8,128)S(1)} %add.7.s0), channel_id=1, source_target_pairs={{0,2},{2,4},{4,6},{6,0},{1,3},{3,5},{5,7},{7,1},{8,10},{10,12},{12... | collective-permute-start | bytes 49160 | tf_op jit(solution)/shard_map/ppermute | solution.py:272

commit v3 on v2

--- a/solution.py
+++ b/solution.py
@@ -18,6 +18,10 @@
 SMEM = pl.BlockSpec(memory_space=pltpu.SMEM)
 HBM = pl.BlockSpec(memory_space=pltpu.HBM)
 CHUNK = 256
+TURN_X = [3, 0, 1, 2]
+TURN_Y = [3, 0, 1, 2]
+TURN_Z = [6, 7, 0, 1, 2, 3, 4, 5]
+HALVES = (slice(0, 128), slice(128, 256))
 
 
 def pieces(v):
@@ -57,19 +61,21 @@
     copies = [pltpu.make_async_copy(signal.at[:, part], held.at[:, part], sems.at[i]) for i, part in enumerate(parts)]
     for copy in copies:
         copy.start()
-    jumps_in = pltpu.make_async_copy(jumps, out.at[0:KD, :], sem2.at[1])
-    jumps_in.start()
+    jumps_in = [pltpu.make_async_copy(jumps.at[:, half], out.at[i * KD : (i + 1) * KD, :], sem2.at[1 + i]) for i, half in enumerate(HALVES)]
+    for copy in jumps_in:
+        copy.start()
     z = lax.axis_index("z")
     start = (lax.axis_index("x") * NZ + z) * width
     sub = lax.broadcasted_iota(jnp.int32, (40, 128), 0)
-    lane = lax.broadcasted_iota(jnp.int32, (8, KZ), 1)
+    lane = lax.broadcasted_iota(jnp.int32, (8, 128), 1)
     at = jnp.where(sub == KD, -1, width)
-    row = jnp.zeros((8, KZ), jnp.int32)
+    row = jnp.zeros((8, 128), jnp.int32)
+    shift = lax.rem(z * KD, 128)
     marks_in.wait()
     for k in range(KD):
         mark = at_smem[k]
         at = jnp.where(sub == k, mark - start, at)
-        row = jnp.where(lane == z * KD + k, mark, row)
+        row = jnp.where(lane == shift + k, mark, row)
     at = jnp.concatenate([at] * (CHUNK // 128), axis=1)
     bin_at = lax.broadcasted_iota(jnp.int32, (40, CHUNK), 1)
     total = jnp.zeros((40, rows), F32)
@@ -78,10 +84,14 @@
         copy.wait()
         for piece in pieces(held[:, part])[::-1]:
             total += lax.dot_general(mask, piece, (((1,), (1,)), ((), ())), preferred_element_type=F32)
-    out[KD : 2 * KD, :] = total[:KD]
-    sub8 = lax.broadcasted_iota(jnp.int32, (8, KZ), 0)
-    out[2 * KD :, :] = jnp.where(sub8 == 1, row.astype(F32), total[KD:])
-    jumps_in.wait()
+    tail = row.astype(F32)
+    sub8 = lax.broadcasted_iota(jnp.int32, (8, 128), 0)
+    for i, half in enumerate(HALVES):
+        out[(2 + i) * KD : (3 + i) * KD, :] = total[:KD, half]
+        tail = jnp.where(sub8 == i, total[KD : KD + 1, half], tail)
+    out[4 * KD :, :] = tail
+    for copy in jumps_in:
+        copy.wait()
 
 
 def gram(after):
@@ -99,18 +109,25 @@
 
 
 def group_sums(bins, got, big, small):
-    head = got[...]
-    after = (bins - 1.0) - column_sum(head[:, 2 * KD + 1, :])
+    at = [TURN_Z.index(z) for z in range(NZ)]
+    marks = [sum(got[at[z], 4 * KD + 2 : 4 * KD + 3, :] for z in range(i * 4, i * 4 + 4)) for i in range(2)]
+    after = (bins - 1.0) - jnp.concatenate(marks, axis=1)
     wide = jnp.broadcast_to(after, (KZ, KZ)).T
     overlap = jnp.minimum(jnp.broadcast_to(after, (KZ, KZ)), wide)
-    jumps = head[:, :KD, :].reshape(KZ, KZ)
-    later = jnp.zeros((1, KZ), F32)
-    behind = [None] * NZ
-    for z in range(NZ - 1, -1, -1):
-        behind[z] = head[z, KD : 2 * KD, :] + later
-        later = later + head[z, 2 * KD : 2 * KD + 1, :]
+    jumps = [jnp.concatenate([got[k, i * KD : (i + 1) * KD, :] for k in at], axis=0) for i in range(2)]
+    jumps = jnp.concatenate(jumps, axis=1)
+    later, behind = [], []
+    for i in range(2):
+        total = jnp.zeros((1, 128), F32)
+        part = [None] * NZ
+        for z in range(NZ - 1, -1, -1):
+            part[z] = got[at[z], (2 + i) * KD : (3 + i) * KD, :] + total
+            total = total + got[at[z], 4 * KD + i : 4 * KD + i + 1, :]
+        later.append(total)
+        behind.append(jnp.concatenate(part, axis=0))
+    later = jnp.concatenate(later, axis=1)
     own = jnp.dot(overlap, jumps, precision=lax.Precision.HIGHEST, preferred_element_type=F32)
-    corr = jnp.concatenate(behind, axis=0) - own
+    corr = jnp.concatenate(behind, axis=1) - own
     small[TOTAL : TOTAL + 1, :] = later
     small[JUMPS : JUMPS + 1, :] = column_sum(jumps)
     small[WEIGHTED : WEIGHTED + 1, :] = column_sum(jumps * wide)
@@ -126,6 +143,10 @@
     return [lax.rem(x + NX - k, NX) for k in range(NX)]
 
 
+def turn_x(k):
+    return lax.rem(k + 1, NX)
+
+
 def weights(place):
     one = lambda c: jnp.where(c, 1.0, 0.0).astype(F32)
     return [[one(place[q] < place[p]) for q in range(NX)] for p in range(NX)]
@@ -148,7 +169,7 @@
 
 def own_stats(big, ms, stats):
     place = places()
-    smalls = [ms.at[k] for k in place]
+    smalls = [ms.at[turn_x(k)] for k in place]
     m0 = smalls[0]
     before = weights(place)
     lower, upper = base_rows(before, smalls)
@@ -188,8 +209,8 @@
 
 def second_corr(b0, b1, b2, b3, ms, ss, jumps_out, corr_out, stats):
     place = places()
-    smalls = [ms.at[k] for k in place]
-    bigs, sums_in = (b0, b1, b2, b3), [ss.at[k] for k in place]
+    smalls = [ms.at[turn_x(k)] for k in place]
+    bigs, sums_in = (b0, b1, b2, b3), [ss.at[turn_x(k)] for k in place]
     before = weights(place)
     after = [m[AFTER : AFTER + 1, :] for m in smalls]
     overlap = [gram(a) for a in after]
@@ -278,22 +299,28 @@
     slab = [pltpu.VMEM((rows, width), F32), pltpu.SemaphoreType.DMA((width // CHUNK,))]
     first = call(
         local_sums,
-        [(2 * KD + 8, rows)],
+        [(4 * KD + 8, rows // 2)],
         [HBM] * 3,
-        scratch=[pltpu.SMEM((KD,), jnp.int32)] + slab + [pltpu.SemaphoreType.DMA((2,))],
+        scratch=[pltpu.SMEM((KD,), jnp.int32)] + slab + [pltpu.SemaphoreType.DMA((3,))],
     )
     (mine,) = first(*[pltpu.with_memory_space_constraint(a, pltpu.HBM) for a in (breaks, signal, jumps.T)])
-    near = lax.all_to_all(jnp.broadcast_to(mine[None], (NZ,) + mine.shape), "z", 0, 0, tiled=False)
+    near = lax.all_to_all(
+        jnp.broadcast_to(mine[None], (NZ,) + mine.shape), "z", 0, 0, axis_index_groups=[TURN_Z], tiled=False
+    )
     big, small = call(functools.partial(group_sums, bins), [(2 * KZ, rows), (8, rows)], [VMEM])(near)
     ring = lambda k: [(i, (i + k) % NX) for i in range(NX)]
     b1, b3 = lax.ppermute(big, "x", ring(1)), lax.ppermute(big, "x", ring(3))
-    smalls = lax.all_to_all(jnp.broadcast_to(small[None], (NX,) + small.shape), "x", 0, 0, tiled=False)
+    smalls = lax.all_to_all(
+        jnp.broadcast_to(small[None], (NX,) + small.shape), "x", 0, 0, axis_index_groups=[TURN_X], tiled=False
+    )
     bg, smalls = lax.optimization_barrier((big, smalls))
     bigs = [big, b1, lax.ppermute(bg, "x", ring(2)), b3]
     (stats,) = call(own_stats, [(8, KZ)], [VMEM] * 2)(big, smalls)
     stats = stats + lax.ppermute(stats, "core", [(0, 1), (1, 0)])
-    stats = lax.all_to_all(jnp.broadcast_to(stats[None], (NY,) + stats.shape), "y", 0, 0, tiled=False).sum(0)
-    sums = lax.all_to_all(jnp.broadcast_to(stats[None], (NX,) + stats.shape), "x", 0, 0, tiled=False)
+    stats = lax.all_to_all(jnp.broadcast_to(stats[None], (NY,) + stats.shape), "y", 0, 0, axis_index_groups=[TURN_Y], tiled=False).sum(0)
+    sums = lax.all_to_all(
+        jnp.broadcast_to(stats[None], (NX,) + stats.shape), "x", 0, 0, axis_index_groups=[TURN_X], tiled=False
+    )
     jumps1, corr, stats = call(second_corr, [(NX, rows, KZ), (NX, rows, KZ), (16, KZ)], [VMEM] * 6)(*bigs, smalls, sums)
     parts = over_samples(stats)
     last = call(functools.partial(finish, bins), [(rows, width), (KD, rows)], [VMEM] * 8, [HBM, VMEM], slab)

time: 77.1 us -> 72.7 us (0.943); the launches traced: 76.8 us -> 71.6 us
  blocking collectives: 44.1 us -> 38.2 us
  starting transfers between devices: 17 us -> 18.1 us
    all_to_all x1, blocking collectives: 26.2 us -> 21.8 us  [body(): lax.all_to_all(jnp.broadcast_to(mine[None], (NZ,) + mine.shape), 'z', 0,...]
    all_to_all x1, starting transfers between devices: 4.01 us -> 5.71 us  [body(): lax.all_to_all(jnp.broadcast_to(small[None], (NX,) + small.shape), 'x', 0...]
    ppermute x2, starting transfers between devices: 2.68 us -> 1.47 us  [body(): b1, b3 = (lax.ppermute(big, 'x', ring(1)), lax.ppermute(big, 'x', ring(3)))]
    ppermute x1, starting transfers between devices: 0.8 us -> 1.78 us  [body(): bigs = [big, b1, lax.ppermute(bg, 'x', ring(2)), b3]]
where the time goes in v3:
time: 72.7 us; the launch traced here: 71.6 us
  blocking collectives  38.2 us (53%)
  starting transfers between devices  18.1 us (25%)
  Pallas kernels  7.92 us (11%)
  waiting for transfers between devices  5.96 us (8%)
    all_to_all x1, blocking collectives, body(): lax.all_to_all(jnp.broadcast_to(mine[None], (NZ,) + mine.shape), 'z', 0,...  21.8 us
    all_to_all x1, blocking collectives, body(): lax.all_to_all(jnp.broadcast_to(stats[None], (NX,) + stats.shape), 'x', 0...  8.79 us
    all_to_all x1, blocking collectives, body(): lax.all_to_all(jnp.broadcast_to(stats[None], (NY,) + stats.shape), 'y', 0...  7.59 us
    all_to_all x1, starting transfers between devices, body(): lax.all_to_all(jnp.broadcast_to(small[None], (NX,) + small.shape), 'x', 0...  5.71 us
    ppermute x1, starting transfers between devices, body(): stats = stats + lax.ppermute(stats, 'core', [(0, 1), (1, 0)])  4.77 us
    ppermute x3, starting transfers between devices, over_samples(): return [stats] + [lax.ppermute(stats, 'y', ring(k)) for k in range(1, NY)]  3.61 us
    ppermute x3, waiting for transfers between devices, over_samples(): return [stats] + [lax.ppermute(stats, 'y', ring(k)) for k in range(1, NY)]  3.23 us
    pallas_call x1, Pallas kernels, body(): resid, jumps2 = last(signal, small, jumps1, corr, *parts)  2.38 us
  transfers between devices with their start and end apart: 9, of which 5 were waited for; matrix products, arithmetic and copies ran while one was open for 0% of the time, Pallas kernels for 1%

profile of v3, /device:TPU:1, one launch (start us, length us, event | category | flops | bytes accessed | tf_op | source)
XLA Modules:
  0.0 71.6 jit_solution(10912946589767908341)
XLA Ops:
  0.6 2.1 %shard_map.50 = f32[136,128]{1,0:T(8,128)S(1)} custom-call(s32[32]{0:T(128)} %breaks.1, f32[256,1024]{1,0:T(8,128)} %signal.3, f32[32,256]{1,0:T(8,128)} %bitcast.2), custom_call_target="tpu_custom_call" | custom-call | tf_op jit(solution)/shard_map/pallas_call | solution.py:306
  2.8 21.8 %all_to_all.20.got = f32[8,136,128]{2,1,0:T(8,128)S(1)} all-to-all(f32[8,136,128]{2,1,0:T(8,128)S(1)} %broadcast_in_dim.8), channel_id=1, replica_groups={{48,56,0,8,16,24,32,40},{49,57,1,9,17,25,33,41},{50,58,2,10,18,26,34,42..., dimensions={0} | all-to-all | bytes 1114112 | tf_op jit(solution)/shard_map/all_to_all | solution.py:307
  24.7 0.5 shard_map.51
  25.2 0.6 broadcast_in_dim.9
  25.8 5.7 %all-to-all-start.1 = ((f32[4,8,256]{2,1,0:T(8,128)}), f32[4,8,256]{2,1,0:T(8,128)S(1)}, u32[]{:S(2)}, u32[]{:S(2)}) async-start(f32[4,8,256]{2,1,0:T(8,128)} %broadcast_in_dim.9), calls=%async_computation.1 | async-start | bytes 65536 | tf_op jit(solution)/shard_map/all_to_all | solution.py:313
  31.5 0.1 collective-permute-start.2
  31.6 1.3 %collective-permute-start = (f32[512,256]{1,0:T(8,128)S(1)}, f32[512,256]{1,0:T(8,128)S(1)}, u32[]{:S(2)}, u32[]{:S(2)}) collective-permute-start(f32[512,256]{1,0:T(8,128)S(1)} %get-tuple-element.13.big.b0), channel_id=1, source_target_pairs={{0,64},{64,128},{128,192},{192,0},{1,65},{65,129},{129,193},{193,1... | collective-permute-start | bytes 1572872 | tf_op jit(solution)/shard_map/ppermute | solution.py:312
  33.0 1.1 %all-to-all-done.1.ms = f32[4,8,256]{2,1,0:T(8,128)S(1)} async-done(((f32[4,8,256]{2,1,0:T(8,128)}), f32[4,8,256]{2,1,0:T(8,128)S(1)}, u32[]{:S(2)}, u32[]{:S(2)}) %all-to-all-start.1) | async-done | bytes 32800 | tf_op jit(solution)/shard_map/all_to_all | solution.py:313
  34.0 1.8 %collective-permute-start.1 = (f32[512,256]{1,0:T(8,128)S(1)}, f32[512,256]{1,0:T(8,128)S(1)}, u32[]{:S(2)}, u32[]{:S(2)}) collective-permute-start(f32[512,256]{1,0:T(8,128)S(1)} %get-tuple-element.13.big.b0), channel_id=1, source_target_pairs={{0,128},{64,192},{128,0},{192,64},{1,129},{65,193},{129,1},{193,65... | collective-permute-start | bytes 1572872 | tf_op jit(solution)/shard_map/ppermute | solution.py:317
  35.8 0.6 shard_map.52
  36.4 4.8 %collective-permute-start.3 = (f32[8,256]{1,0:T(8,128)S(1)}, f32[8,256]{1,0:T(8,128)S(1)}, u32[]{:S(2)}, u32[]{:S(2)}) collective-permute-start(f32[8,256]{1,0:T(8,128)S(1)} %shard_map.52), channel_id=1, source_target_pairs={{0,1},{1,0},{2,3},{3,2},{4,5},{5,4},{6,7},{7,6},{8,9},{9,8},{10,11... | collective-permute-start | bytes 24584 | tf_op jit(solution)/shard_map/ppermute | solution.py:319
  41.2 0.8 %collective-permute-done.3 = f32[8,256]{1,0:T(8,128)S(1)} collective-permute-done((f32[8,256]{1,0:T(8,128)S(1)}, f32[8,256]{1,0:T(8,128)S(1)}, u32[]{:S(2)}, u32[]{:S(2)}) %collective-permute-start.3) | collective-permute-done | bytes 8224 | tf_op jit(solution)/shard_map/ppermute | solution.py:319
  42.0 7.6 %all_to_all.21 = f32[4,8,256]{2,1,0:T(8,128)S(1)} all-to-all(f32[4,8,256]{2,1,0:T(8,128)S(1)} %broadcast_in_dim.10), channel_id=1, replica_groups={{6,0,2,4},{7,1,3,5},{14,8,10,12},{15,9,11,13},{22,16,18,20},{23,17,19,2..., dimensions={0} | all-to-all | bytes 65536 | tf_op jit(solution)/shard_map/all_to_all | solution.py:320
  49.6 8.8 %all_to_all.22.ss = f32[4,8,256]{2,1,0:T(8,128)S(1)} all-to-all(f32[4,8,256]{2,1,0:T(8,128)S(1)} %broadcast_in_dim.11), channel_id=1, replica_groups={{192,0,64,128},{193,1,65,129},{194,2,66,130},{195,3,67,131},{196,4,68,1..., dimensions={0} | all-to-all | bytes 65536 | tf_op jit(solution)/shard_map/all_to_all | solution.py:321
  58.4 0.0 collective-permute-done.b1
  58.4 2.3 %shard_map.53 = (f32[4,256,256]{2,1,0:T(8,128)S(1)}, f32[4,256,256]{2,1,0:T(8,128)S(1)}, f32[16,256]{1,0:T(8,128)S(1)}) custom-call(f32[512,256]{1,0:T(8,128)S(1)} %get-tuple-element.13.big.b0, f32[512,256]{1,0:T(8,128)S(1)} %collective-permute-done.b1, f32[512,256]{1,0:T(8,128)S(1)} %collective-permute-done.1.b2, f32[512,256]{1,0:T(8,128)S(1)} %collective-permute-done.2.b3, ...), custom_call_target="tpu_custom_call" | custom-call | tf_op jit(solution)/shard_map/pallas_call | solution.py:324
  60.7 0.8 %collective-permute-start.4 = (f32[16,256]{1,0:T(8,128)S(1)}, f32[16,256]{1,0:T(8,128)S(1)}, u32[]{:S(2)}, u32[]{:S(2)}) collective-permute-start(f32[16,256]{1,0:T(8,128)S(1)} %get-tuple-element.17), channel_id=1, source_target_pairs={{0,1},{1,0},{2,3},{3,2},{4,5},{5,4},{6,7},{7,6},{8,9},{9,8},{10,11... | collective-permute-start | bytes 49160 | tf_op jit(solution)/shard_map/ppermute | solution.py:291
  61.5 0.8 %collective-permute-done.4 = f32[16,256]{1,0:T(8,128)S(1)} collective-permute-done((f32[16,256]{1,0:T(8,128)S(1)}, f32[16,256]{1,0:T(8,128)S(1)}, u32[]{:S(2)}, u32[]{:S(2)}) %collective-permute-start.4) | collective-permute-done | bytes 16416 | tf_op jit(solution)/shard_map/ppermute | solution.py:291
  62.4 2.6 %collective-permute-start.7 = (f32[16,256]{1,0:T(8,128)S(1)}, f32[16,256]{1,0:T(8,128)S(1)}, u32[]{:S(2)}, u32[]{:S(2)}) collective-permute-start(f32[16,256]{1,0:T(8,128)S(1)} %add.7.s0), channel_id=1, source_target_pairs={{0,6},{2,0},{4,2},{6,4},{1,7},{3,1},{5,3},{7,5},{8,14},{10,8},{12,... | collective-permute-start | bytes 49160 | tf_op jit(solution)/shard_map/ppermute | solution.py:293
  64.9 0.3 collective-permute-start.6
  65.3 0.7 collective-permute-start.5
  66.0 3.1 %collective-permute-done.6.s2 = f32[16,256]{1,0:T(8,128)S(1)} collective-permute-done((f32[16,256]{1,0:T(8,128)S(1)}, f32[16,256]{1,0:T(8,128)S(1)}, u32[]{:S(2)}, u32[]{:S(2)}) %collective-permute-start.6) | collective-permute-done | bytes 16416 | tf_op jit(solution)/shard_map/ppermute | solution.py:293
  69.0 0.2 collective-permute-done.5.s1
  69.2 2.4 %shard_map.54 = (f32[256,1024]{1,0:T(8,128)}, f32[32,256]{1,0:T(8,128)}) custom-call(f32[256,1024]{1,0:T(8,128)S(1)} %copy-done, f32[8,256]{1,0:T(8,128)S(1)} %get-tuple-element.11.m0, f32[4,256,256]{2,1,0:T(8,128)S(1)} %get-tuple-element.15.jumps_in, f32[4,256,256]{2,1,0:T(8,128)S(1)} %get-tuple-element.16.corr_in, f32[16,256]{1,0:T(8,128)S(1)} %add.7.s0, ...), custom_call_target="tpu_custom_call" | custom-call | tf_op jit(solution)/shard_map/pallas_call | solution.py:327
  (11 shorter events, 0.1 us)
Async XLA Ops:
  25.8 8.2 %all-to-all-start.1 = ((f32[4,8,256]{2,1,0:T(8,128)}), f32[4,8,256]{2,1,0:T(8,128)S(1)}, u32[]{:S(2)}, u32[]{:S(2)}) async-start(f32[4,8,256]{2,1,0:T(8,128)} %broadcast_in_dim.9), calls=%async_computation.1 | async-start | bytes 65536 | tf_op jit(solution)/shard_map/all_to_all | solution.py:313
  31.5 26.9 %collective-permute-start.2 = (f32[512,256]{1,0:T(8,128)S(1)}, f32[512,256]{1,0:T(8,128)S(1)}, u32[]{:S(2)}, u32[]{:S(2)}) collective-permute-start(f32[512,256]{1,0:T(8,128)S(1)} %get-tuple-element.13.big.b0), channel_id=1, source_target_pairs={{0,192},{64,0},{128,64},{192,128},{1,193},{65,1},{129,65},{193,129... | collective-permute-start | bytes 1572872 | tf_op jit(solution)/shard_map/ppermute | solution.py:312
  31.6 26.8 %collective-permute-start = (f32[512,256]{1,0:T(8,128)S(1)}, f32[512,256]{1,0:T(8,128)S(1)}, u32[]{:S(2)}, u32[]{:S(2)}) collective-permute-start(f32[512,256]{1,0:T(8,128)S(1)} %get-tuple-element.13.big.b0), channel_id=1, source_target_pairs={{0,64},{64,128},{128,192},{192,0},{1,65},{65,129},{129,193},{193,1... | collective-permute-start | bytes 1572872 | tf_op jit(solution)/shard_map/ppermute | solution.py:312
  34.0 24.4 %collective-permute-start.1 = (f32[512,256]{1,0:T(8,128)S(1)}, f32[512,256]{1,0:T(8,128)S(1)}, u32[]{:S(2)}, u32[]{:S(2)}) collective-permute-start(f32[512,256]{1,0:T(8,128)S(1)} %get-tuple-element.13.big.b0), channel_id=1, source_target_pairs={{0,128},{64,192},{128,0},{192,64},{1,129},{65,193},{129,1},{193,65... | collective-permute-start | bytes 1572872 | tf_op jit(solution)/shard_map/ppermute | solution.py:317
  36.4 5.6 %collective-permute-start.3 = (f32[8,256]{1,0:T(8,128)S(1)}, f32[8,256]{1,0:T(8,128)S(1)}, u32[]{:S(2)}, u32[]{:S(2)}) collective-permute-start(f32[8,256]{1,0:T(8,128)S(1)} %shard_map.52), channel_id=1, source_target_pairs={{0,1},{1,0},{2,3},{3,2},{4,5},{5,4},{6,7},{7,6},{8,9},{9,8},{10,11... | collective-permute-start | bytes 24584 | tf_op jit(solution)/shard_map/ppermute | solution.py:319
  58.4 10.8 %copy-start = (f32[256,1024]{1,0:T(8,128)S(1)}, f32[256,1024]{1,0:T(8,128)}, u32[]{:S(2)}) copy-start(f32[256,1024]{1,0:T(8,128)} %signal.3) | copy-start | bytes 3145732
  60.7 1.6 %collective-permute-start.4 = (f32[16,256]{1,0:T(8,128)S(1)}, f32[16,256]{1,0:T(8,128)S(1)}, u32[]{:S(2)}, u32[]{:S(2)}) collective-permute-start(f32[16,256]{1,0:T(8,128)S(1)} %get-tuple-element.17), channel_id=1, source_target_pairs={{0,1},{1,0},{2,3},{3,2},{4,5},{5,4},{6,7},{7,6},{8,9},{9,8},{10,11... | collective-permute-start | bytes 49160 | tf_op jit(solution)/shard_map/ppermute | solution.py:291
  62.4 3.6 %collective-permute-start.7 = (f32[16,256]{1,0:T(8,128)S(1)}, f32[16,256]{1,0:T(8,128)S(1)}, u32[]{:S(2)}, u32[]{:S(2)}) collective-permute-start(f32[16,256]{1,0:T(8,128)S(1)} %add.7.s0), channel_id=1, source_target_pairs={{0,6},{2,0},{4,2},{6,4},{1,7},{3,1},{5,3},{7,5},{8,14},{10,8},{12,... | collective-permute-start | bytes 49160 | tf_op jit(solution)/shard_map/ppermute | solution.py:293
  64.9 4.1 %collective-permute-start.6 = (f32[16,256]{1,0:T(8,128)S(1)}, f32[16,256]{1,0:T(8,128)S(1)}, u32[]{:S(2)}, u32[]{:S(2)}) collective-permute-start(f32[16,256]{1,0:T(8,128)S(1)} %add.7.s0), channel_id=1, source_target_pairs={{0,4},{2,6},{4,0},{6,2},{1,5},{3,7},{5,1},{7,3},{8,12},{10,14},{12... | collective-permute-start | bytes 49160 | tf_op jit(solution)/shard_map/ppermute | solution.py:293
  65.3 3.9 %collective-permute-start.5 = (f32[16,256]{1,0:T(8,128)S(1)}, f32[16,256]{1,0:T(8,128)S(1)}, u32[]{:S(2)}, u32[]{:S(2)}) collective-permute-start(f32[16,256]{1,0:T(8,128)S(1)} %add.7.s0), channel_id=1, source_target_pairs={{0,2},{2,4},{4,6},{6,0},{1,3},{3,5},{5,7},{7,1},{8,10},{10,12},{12... | collective-permute-start | bytes 49160 | tf_op jit(solution)/shard_map/ppermute | solution.py:293

commit v4 on v3

--- a/solution.py
+++ b/solution.py
@@ -19,7 +19,7 @@
 HBM = pl.BlockSpec(memory_space=pltpu.HBM)
 CHUNK = 256
 TURN_X = [3, 0, 1, 2]
-TURN_Y = [3, 0, 1, 2]
+TURN_Y = [2, 3, 0, 1]
 TURN_Z = [6, 7, 0, 1, 2, 3, 4, 5]
 HALVES = (slice(0, 128), slice(128, 256))
 
@@ -289,8 +289,7 @@
 
 def over_samples(stats):
     stats = stats + lax.ppermute(stats, "core", [(0, 1), (1, 0)])
-    ring = lambda k: [(i, (i + k) % NY) for i in range(NY)]
-    return [stats] + [lax.ppermute(stats, "y", ring(k)) for k in range(1, NY)]
+    return [stats] + [lax.ppermute(stats, "y", [(i, i ^ k) for i in range(NY)]) for k in (1, 2, 3)]
 
 
 def body(signal, jumps, breaks):

time: 72.7 us -> 72.4 us (level)
  no operation moved by 1% of the time
where the time goes in v4:
time: 72.4 us; the launch traced here: 71.4 us
  blocking collectives  38.3 us (53%)
  starting transfers between devices  17.6 us (24%)
  Pallas kernels  7.92 us (11%)
  waiting for transfers between devices  6.18 us (9%)
    all_to_all x1, blocking collectives, body(): lax.all_to_all(jnp.broadcast_to(mine[None], (NZ,) + mine.shape), 'z', 0,...  21.8 us
    all_to_all x1, blocking collectives, body(): lax.all_to_all(jnp.broadcast_to(stats[None], (NX,) + stats.shape), 'x', 0...  9.42 us
    all_to_all x1, blocking collectives, body(): lax.all_to_all(jnp.broadcast_to(stats[None], (NY,) + stats.shape), 'y', 0...  7.07 us
    all_to_all x1, starting transfers between devices, body(): lax.all_to_all(jnp.broadcast_to(small[None], (NX,) + small.shape), 'x', 0...  5.71 us
    ppermute x1, starting transfers between devices, body(): stats = stats + lax.ppermute(stats, 'core', [(0, 1), (1, 0)])  4.77 us
    ppermute x3, waiting for transfers between devices, over_samples(): lax.ppermute(stats, 'y', [(i, i ^ k) for i in range(NY)])  3.45 us
    ppermute x3, starting transfers between devices, over_samples(): lax.ppermute(stats, 'y', [(i, i ^ k) for i in range(NY)])  3.38 us
    pallas_call x1, Pallas kernels, body(): resid, jumps2 = last(signal, small, jumps1, corr, *parts)  2.38 us
  transfers between devices with their start and end apart: 9, of which 5 were waited for; matrix products, arithmetic and copies ran while one was open for 0% of the time, Pallas kernels for 1%

profile of v4, /device:TPU:1, one launch (start us, length us, event | category | flops | bytes accessed | tf_op | source)
XLA Modules:
  0.0 71.4 jit_solution(8880428883048995915)
XLA Ops:
  0.6 2.1 %shard_map.50 = f32[136,128]{1,0:T(8,128)S(1)} custom-call(s32[32]{0:T(128)} %breaks.1, f32[256,1024]{1,0:T(8,128)} %signal.3, f32[32,256]{1,0:T(8,128)} %bitcast.2), custom_call_target="tpu_custom_call" | custom-call | tf_op jit(solution)/shard_map/pallas_call | solution.py:305
  2.8 21.8 %all_to_all.20.got = f32[8,136,128]{2,1,0:T(8,128)S(1)} all-to-all(f32[8,136,128]{2,1,0:T(8,128)S(1)} %broadcast_in_dim.8), channel_id=1, replica_groups={{48,56,0,8,16,24,32,40},{49,57,1,9,17,25,33,41},{50,58,2,10,18,26,34,42..., dimensions={0} | all-to-all | bytes 1114112 | tf_op jit(solution)/shard_map/all_to_all | solution.py:306
  24.7 0.5 shard_map.51
  25.2 0.6 broadcast_in_dim.9
  25.8 5.7 %all-to-all-start.1 = ((f32[4,8,256]{2,1,0:T(8,128)}), f32[4,8,256]{2,1,0:T(8,128)S(1)}, u32[]{:S(2)}, u32[]{:S(2)}) async-start(f32[4,8,256]{2,1,0:T(8,128)} %broadcast_in_dim.9), calls=%async_computation.1 | async-start | bytes 65536 | tf_op jit(solution)/shard_map/all_to_all | solution.py:312
  31.5 0.1 collective-permute-start.2
  31.6 1.3 %collective-permute-start = (f32[512,256]{1,0:T(8,128)S(1)}, f32[512,256]{1,0:T(8,128)S(1)}, u32[]{:S(2)}, u32[]{:S(2)}) collective-permute-start(f32[512,256]{1,0:T(8,128)S(1)} %get-tuple-element.13.big.b0), channel_id=1, source_target_pairs={{0,64},{64,128},{128,192},{192,0},{1,65},{65,129},{129,193},{193,1... | collective-permute-start | bytes 1572872 | tf_op jit(solution)/shard_map/ppermute | solution.py:311
  33.0 1.1 %all-to-all-done.1.ms = f32[4,8,256]{2,1,0:T(8,128)S(1)} async-done(((f32[4,8,256]{2,1,0:T(8,128)}), f32[4,8,256]{2,1,0:T(8,128)S(1)}, u32[]{:S(2)}, u32[]{:S(2)}) %all-to-all-start.1) | async-done | bytes 32800 | tf_op jit(solution)/shard_map/all_to_all | solution.py:312
  34.0 1.8 %collective-permute-start.1 = (f32[512,256]{1,0:T(8,128)S(1)}, f32[512,256]{1,0:T(8,128)S(1)}, u32[]{:S(2)}, u32[]{:S(2)}) collective-permute-start(f32[512,256]{1,0:T(8,128)S(1)} %get-tuple-element.13.big.b0), channel_id=1, source_target_pairs={{0,128},{64,192},{128,0},{192,64},{1,129},{65,193},{129,1},{193,65... | collective-permute-start | bytes 1572872 | tf_op jit(solution)/shard_map/ppermute | solution.py:316
  35.8 0.6 shard_map.52
  36.4 4.8 %collective-permute-start.3 = (f32[8,256]{1,0:T(8,128)S(1)}, f32[8,256]{1,0:T(8,128)S(1)}, u32[]{:S(2)}, u32[]{:S(2)}) collective-permute-start(f32[8,256]{1,0:T(8,128)S(1)} %shard_map.52), channel_id=1, source_target_pairs={{0,1},{1,0},{2,3},{3,2},{4,5},{5,4},{6,7},{7,6},{8,9},{9,8},{10,11... | collective-permute-start | bytes 24584 | tf_op jit(solution)/shard_map/ppermute | solution.py:318
  41.2 0.8 %collective-permute-done.3 = f32[8,256]{1,0:T(8,128)S(1)} collective-permute-done((f32[8,256]{1,0:T(8,128)S(1)}, f32[8,256]{1,0:T(8,128)S(1)}, u32[]{:S(2)}, u32[]{:S(2)}) %collective-permute-start.3) | collective-permute-done | bytes 8224 | tf_op jit(solution)/shard_map/ppermute | solution.py:318
  42.0 7.1 %all_to_all.21 = f32[4,8,256]{2,1,0:T(8,128)S(1)} all-to-all(f32[4,8,256]{2,1,0:T(8,128)S(1)} %broadcast_in_dim.10), channel_id=1, replica_groups={{4,6,0,2},{5,7,1,3},{12,14,8,10},{13,15,9,11},{20,22,16,18},{21,23,17,1..., dimensions={0} | all-to-all | bytes 65536 | tf_op jit(solution)/shard_map/all_to_all | solution.py:319
  49.1 9.4 %all_to_all.22.ss = f32[4,8,256]{2,1,0:T(8,128)S(1)} all-to-all(f32[4,8,256]{2,1,0:T(8,128)S(1)} %broadcast_in_dim.11), channel_id=1, replica_groups={{192,0,64,128},{193,1,65,129},{194,2,66,130},{195,3,67,131},{196,4,68,1..., dimensions={0} | all-to-all | bytes 65536 | tf_op jit(solution)/shard_map/all_to_all | solution.py:320
  58.5 0.0 collective-permute-done.2.b3
  58.5 2.3 %shard_map.53 = (f32[4,256,256]{2,1,0:T(8,128)S(1)}, f32[4,256,256]{2,1,0:T(8,128)S(1)}, f32[16,256]{1,0:T(8,128)S(1)}) custom-call(f32[512,256]{1,0:T(8,128)S(1)} %get-tuple-element.13.big.b0, f32[512,256]{1,0:T(8,128)S(1)} %collective-permute-done.b1, f32[512,256]{1,0:T(8,128)S(1)} %collective-permute-done.1.b2, f32[512,256]{1,0:T(8,128)S(1)} %collective-permute-done.2.b3, ...), custom_call_target="tpu_custom_call" | custom-call | tf_op jit(solution)/shard_map/pallas_call | solution.py:323
  60.9 0.5 collective-permute-start.4
  61.4 0.8 %collective-permute-done.4 = f32[16,256]{1,0:T(8,128)S(1)} collective-permute-done((f32[16,256]{1,0:T(8,128)S(1)}, f32[16,256]{1,0:T(8,128)S(1)}, u32[]{:S(2)}, u32[]{:S(2)}) %collective-permute-start.4) | collective-permute-done | bytes 16416 | tf_op jit(solution)/shard_map/ppermute | solution.py:291
  62.2 2.7 %collective-permute-start.7 = (f32[16,256]{1,0:T(8,128)S(1)}, f32[16,256]{1,0:T(8,128)S(1)}, u32[]{:S(2)}, u32[]{:S(2)}) collective-permute-start(f32[16,256]{1,0:T(8,128)S(1)} %add.7.s0), channel_id=1, source_target_pairs={{0,6},{2,4},{4,2},{6,0},{1,7},{3,5},{5,3},{7,1},{8,14},{10,12},{12... | collective-permute-start | bytes 49160 | tf_op jit(solution)/shard_map/ppermute | solution.py:292
  64.9 0.3 collective-permute-start.6
  65.3 0.3 collective-permute-start.5
  65.6 0.5 collective-permute-done.7.s3
  66.1 3.0 %collective-permute-done.6.s2 = f32[16,256]{1,0:T(8,128)S(1)} collective-permute-done((f32[16,256]{1,0:T(8,128)S(1)}, f32[16,256]{1,0:T(8,128)S(1)}, u32[]{:S(2)}, u32[]{:S(2)}) %collective-permute-start.6) | collective-permute-done | bytes 16416 | tf_op jit(solution)/shard_map/ppermute | solution.py:292
  69.0 2.4 %shard_map.54 = (f32[256,1024]{1,0:T(8,128)}, f32[32,256]{1,0:T(8,128)}) custom-call(f32[256,1024]{1,0:T(8,128)S(1)} %copy-done, f32[8,256]{1,0:T(8,128)S(1)} %get-tuple-element.11.m0, f32[4,256,256]{2,1,0:T(8,128)S(1)} %get-tuple-element.15.jumps_in, f32[4,256,256]{2,1,0:T(8,128)S(1)} %get-tuple-element.16.corr_in, f32[16,256]{1,0:T(8,128)S(1)} %add.7.s0, ...), custom_call_target="tpu_custom_call" | custom-call | tf_op jit(solution)/shard_map/pallas_call | solution.py:326
  (11 shorter events, 0.1 us)
Async XLA Ops:
  25.8 8.2 %all-to-all-start.1 = ((f32[4,8,256]{2,1,0:T(8,128)}), f32[4,8,256]{2,1,0:T(8,128)S(1)}, u32[]{:S(2)}, u32[]{:S(2)}) async-start(f32[4,8,256]{2,1,0:T(8,128)} %broadcast_in_dim.9), calls=%async_computation.1 | async-start | bytes 65536 | tf_op jit(solution)/shard_map/all_to_all | solution.py:312
  31.5 27.0 %collective-permute-start.2 = (f32[512,256]{1,0:T(8,128)S(1)}, f32[512,256]{1,0:T(8,128)S(1)}, u32[]{:S(2)}, u32[]{:S(2)}) collective-permute-start(f32[512,256]{1,0:T(8,128)S(1)} %get-tuple-element.13.big.b0), channel_id=1, source_target_pairs={{0,192},{64,0},{128,64},{192,128},{1,193},{65,1},{129,65},{193,129... | collective-permute-start | bytes 1572872 | tf_op jit(solution)/shard_map/ppermute | solution.py:311
  31.6 26.9 %collective-permute-start = (f32[512,256]{1,0:T(8,128)S(1)}, f32[512,256]{1,0:T(8,128)S(1)}, u32[]{:S(2)}, u32[]{:S(2)}) collective-permute-start(f32[512,256]{1,0:T(8,128)S(1)} %get-tuple-element.13.big.b0), channel_id=1, source_target_pairs={{0,64},{64,128},{128,192},{192,0},{1,65},{65,129},{129,193},{193,1... | collective-permute-start | bytes 1572872 | tf_op jit(solution)/shard_map/ppermute | solution.py:311
  34.0 24.5 %collective-permute-start.1 = (f32[512,256]{1,0:T(8,128)S(1)}, f32[512,256]{1,0:T(8,128)S(1)}, u32[]{:S(2)}, u32[]{:S(2)}) collective-permute-start(f32[512,256]{1,0:T(8,128)S(1)} %get-tuple-element.13.big.b0), channel_id=1, source_target_pairs={{0,128},{64,192},{128,0},{192,64},{1,129},{65,193},{129,1},{193,65... | collective-permute-start | bytes 1572872 | tf_op jit(solution)/shard_map/ppermute | solution.py:316
  36.4 5.6 %collective-permute-start.3 = (f32[8,256]{1,0:T(8,128)S(1)}, f32[8,256]{1,0:T(8,128)S(1)}, u32[]{:S(2)}, u32[]{:S(2)}) collective-permute-start(f32[8,256]{1,0:T(8,128)S(1)} %shard_map.52), channel_id=1, source_target_pairs={{0,1},{1,0},{2,3},{3,2},{4,5},{5,4},{6,7},{7,6},{8,9},{9,8},{10,11... | collective-permute-start | bytes 24584 | tf_op jit(solution)/shard_map/ppermute | solution.py:318
  58.5 10.5 %copy-start = (f32[256,1024]{1,0:T(8,128)S(1)}, f32[256,1024]{1,0:T(8,128)}, u32[]{:S(2)}) copy-start(f32[256,1024]{1,0:T(8,128)} %signal.3) | copy-start | bytes 3145732
  60.9 1.3 %collective-permute-start.4 = (f32[16,256]{1,0:T(8,128)S(1)}, f32[16,256]{1,0:T(8,128)S(1)}, u32[]{:S(2)}, u32[]{:S(2)}) collective-permute-start(f32[16,256]{1,0:T(8,128)S(1)} %get-tuple-element.17), channel_id=1, source_target_pairs={{0,1},{1,0},{2,3},{3,2},{4,5},{5,4},{6,7},{7,6},{8,9},{9,8},{10,11... | collective-permute-start | bytes 49160 | tf_op jit(solution)/shard_map/ppermute | solution.py:291
  62.2 3.9 %collective-permute-start.7 = (f32[16,256]{1,0:T(8,128)S(1)}, f32[16,256]{1,0:T(8,128)S(1)}, u32[]{:S(2)}, u32[]{:S(2)}) collective-permute-start(f32[16,256]{1,0:T(8,128)S(1)} %add.7.s0), channel_id=1, source_target_pairs={{0,6},{2,4},{4,2},{6,0},{1,7},{3,5},{5,3},{7,1},{8,14},{10,12},{12... | collective-permute-start | bytes 49160 | tf_op jit(solution)/shard_map/ppermute | solution.py:292
  64.9 4.1 %collective-permute-start.6 = (f32[16,256]{1,0:T(8,128)S(1)}, f32[16,256]{1,0:T(8,128)S(1)}, u32[]{:S(2)}, u32[]{:S(2)}) collective-permute-start(f32[16,256]{1,0:T(8,128)S(1)} %add.7.s0), channel_id=1, source_target_pairs={{0,4},{2,6},{4,0},{6,2},{1,5},{3,7},{5,1},{7,3},{8,12},{10,14},{12... | collective-permute-start | bytes 49160 | tf_op jit(solution)/shard_map/ppermute | solution.py:292
  65.3 3.7 %collective-permute-start.5 = (f32[16,256]{1,0:T(8,128)S(1)}, f32[16,256]{1,0:T(8,128)S(1)}, u32[]{:S(2)}, u32[]{:S(2)}) collective-permute-start(f32[16,256]{1,0:T(8,128)S(1)} %add.7.s0), channel_id=1, source_target_pairs={{0,2},{2,0},{4,6},{6,4},{1,3},{3,1},{5,7},{7,5},{8,10},{10,8},{12,... | collective-permute-start | bytes 49160 | tf_op jit(solution)/shard_map/ppermute | solution.py:292

commit v5 on v4

--- a/solution.py
+++ b/solution.py
@@ -312,9 +312,9 @@
     smalls = lax.all_to_all(
         jnp.broadcast_to(small[None], (NX,) + small.shape), "x", 0, 0, axis_index_groups=[TURN_X], tiled=False
     )
-    bg, smalls = lax.optimization_barrier((big, smalls))
-    bigs = [big, b1, lax.ppermute(bg, "x", ring(2)), b3]
     (stats,) = call(own_stats, [(8, KZ)], [VMEM] * 2)(big, smalls)
+    late, stats = lax.optimization_barrier((big, stats))
+    bigs = [big, b1, lax.ppermute(late, "x", ring(2)), b3]
     stats = stats + lax.ppermute(stats, "core", [(0, 1), (1, 0)])
     stats = lax.all_to_all(jnp.broadcast_to(stats[None], (NY,) + stats.shape), "y", 0, 0, axis_index_groups=[TURN_Y], tiled=False).sum(0)
     sums = lax.all_to_all(

time: 72.4 us -> 72.4 us (level)
  no operation moved by 1% of the time
where the time goes in v5:
time: 72.4 us; the launch traced here: 71.4 us
  blocking collectives  38.3 us (53%)
  starting transfers between devices  17.6 us (24%)
  Pallas kernels  7.92 us (11%)
  waiting for transfers between devices  6.18 us (9%)
    all_to_all x1, blocking collectives, body(): lax.all_to_all(jnp.broadcast_to(mine[None], (NZ,) + mine.shape), 'z', 0,...  21.8 us
    all_to_all x1, blocking collectives, body(): lax.all_to_all(jnp.broadcast_to(stats[None], (NX,) + stats.shape), 'x', 0...  9.42 us
    all_to_all x1, blocking collectives, body(): lax.all_to_all(jnp.broadcast_to(stats[None], (NY,) + stats.shape), 'y', 0...  7.07 us
    all_to_all x1, starting transfers between devices, body(): lax.all_to_all(jnp.broadcast_to(small[None], (NX,) + small.shape), 'x', 0...  5.71 us
    ppermute x1, starting transfers between devices, body(): stats = stats + lax.ppermute(stats, 'core', [(0, 1), (1, 0)])  4.68 us
    ppermute x3, waiting for transfers between devices, over_samples(): lax.ppermute(stats, 'y', [(i, i ^ k) for i in range(NY)])  3.45 us
    ppermute x3, starting transfers between devices, over_samples(): lax.ppermute(stats, 'y', [(i, i ^ k) for i in range(NY)])  3.38 us
    pallas_call x1, Pallas kernels, body(): resid, jumps2 = last(signal, small, jumps1, corr, *parts)  2.38 us
  transfers between devices with their start and end apart: 9, of which 5 were waited for; matrix products, arithmetic and copies ran while one was open for 0% of the time, Pallas kernels for 1%

profile of v5, /device:TPU:1, one launch (start us, length us, event | category | flops | bytes accessed | tf_op | source)
XLA Modules:
  0.0 71.4 jit_solution(13111168068037310406)
XLA Ops:
  0.6 2.1 %shard_map.50 = f32[136,128]{1,0:T(8,128)S(1)} custom-call(s32[32]{0:T(128)} %breaks.1, f32[256,1024]{1,0:T(8,128)} %signal.3, f32[32,256]{1,0:T(8,128)} %bitcast.2), custom_call_target="tpu_custom_call" | custom-call | tf_op jit(solution)/shard_map/pallas_call | solution.py:305
  2.8 21.8 %all_to_all.20.got = f32[8,136,128]{2,1,0:T(8,128)S(1)} all-to-all(f32[8,136,128]{2,1,0:T(8,128)S(1)} %broadcast_in_dim.8), channel_id=1, replica_groups={{48,56,0,8,16,24,32,40},{49,57,1,9,17,25,33,41},{50,58,2,10,18,26,34,42..., dimensions={0} | all-to-all | bytes 1114112 | tf_op jit(solution)/shard_map/all_to_all | solution.py:306
  24.7 0.5 shard_map.51
  25.2 0.6 broadcast_in_dim.9
  25.8 5.7 %all-to-all-start.1 = ((f32[4,8,256]{2,1,0:T(8,128)}), f32[4,8,256]{2,1,0:T(8,128)S(1)}, u32[]{:S(2)}, u32[]{:S(2)}) async-start(f32[4,8,256]{2,1,0:T(8,128)} %broadcast_in_dim.9), calls=%async_computation.1 | async-start | bytes 65536 | tf_op jit(solution)/shard_map/all_to_all | solution.py:312
  31.5 0.1 collective-permute-start.2
  31.6 1.3 %collective-permute-start = (f32[512,256]{1,0:T(8,128)S(1)}, f32[512,256]{1,0:T(8,128)S(1)}, u32[]{:S(2)}, u32[]{:S(2)}) collective-permute-start(f32[512,256]{1,0:T(8,128)S(1)} %get-tuple-element.13.big.b0), channel_id=1, source_target_pairs={{0,64},{64,128},{128,192},{192,0},{1,65},{65,129},{129,193},{193,1... | collective-permute-start | bytes 1572872 | tf_op jit(solution)/shard_map/ppermute | solution.py:311
  33.0 1.1 %all-to-all-done.1.ms = f32[4,8,256]{2,1,0:T(8,128)S(1)} async-done(((f32[4,8,256]{2,1,0:T(8,128)}), f32[4,8,256]{2,1,0:T(8,128)S(1)}, u32[]{:S(2)}, u32[]{:S(2)}) %all-to-all-start.1) | async-done | bytes 32800 | tf_op jit(solution)/shard_map/all_to_all | solution.py:312
  34.0 0.6 shard_map.52
  34.6 1.9 %collective-permute-start.1 = (f32[512,256]{1,0:T(8,128)S(1)}, f32[512,256]{1,0:T(8,128)S(1)}, u32[]{:S(2)}, u32[]{:S(2)}) collective-permute-start(f32[512,256]{1,0:T(8,128)S(1)} %get-tuple-element.13.big.b0), channel_id=1, source_target_pairs={{0,128},{64,192},{128,0},{192,64},{1,129},{65,193},{129,1},{193,65... | collective-permute-start | bytes 1572872 | tf_op jit(solution)/shard_map/ppermute | solution.py:317
  36.5 4.7 %collective-permute-start.3 = (f32[8,256]{1,0:T(8,128)S(1)}, f32[8,256]{1,0:T(8,128)S(1)}, u32[]{:S(2)}, u32[]{:S(2)}) collective-permute-start(f32[8,256]{1,0:T(8,128)S(1)} %shard_map.52), channel_id=1, source_target_pairs={{0,1},{1,0},{2,3},{3,2},{4,5},{5,4},{6,7},{7,6},{8,9},{9,8},{10,11... | collective-permute-start | bytes 24584 | tf_op jit(solution)/shard_map/ppermute | solution.py:318
  41.2 0.8 %collective-permute-done.3 = f32[8,256]{1,0:T(8,128)S(1)} collective-permute-done((f32[8,256]{1,0:T(8,128)S(1)}, f32[8,256]{1,0:T(8,128)S(1)}, u32[]{:S(2)}, u32[]{:S(2)}) %collective-permute-start.3) | collective-permute-done | bytes 8224 | tf_op jit(solution)/shard_map/ppermute | solution.py:318
  42.0 7.1 %all_to_all.21 = f32[4,8,256]{2,1,0:T(8,128)S(1)} all-to-all(f32[4,8,256]{2,1,0:T(8,128)S(1)} %broadcast_in_dim.10), channel_id=1, replica_groups={{4,6,0,2},{5,7,1,3},{12,14,8,10},{13,15,9,11},{20,22,16,18},{21,23,17,1..., dimensions={0} | all-to-all | bytes 65536 | tf_op jit(solution)/shard_map/all_to_all | solution.py:319
  49.1 9.4 %all_to_all.22.ss = f32[4,8,256]{2,1,0:T(8,128)S(1)} all-to-all(f32[4,8,256]{2,1,0:T(8,128)S(1)} %broadcast_in_dim.11), channel_id=1, replica_groups={{192,0,64,128},{193,1,65,129},{194,2,66,130},{195,3,67,131},{196,4,68,1..., dimensions={0} | all-to-all | bytes 65536 | tf_op jit(solution)/shard_map/all_to_all | solution.py:320
  58.5 0.0 collective-permute-done.2.b3
  58.5 2.3 %shard_map.53 = (f32[4,256,256]{2,1,0:T(8,128)S(1)}, f32[4,256,256]{2,1,0:T(8,128)S(1)}, f32[16,256]{1,0:T(8,128)S(1)}) custom-call(f32[512,256]{1,0:T(8,128)S(1)} %get-tuple-element.13.big.b0, f32[512,256]{1,0:T(8,128)S(1)} %collective-permute-done.b1, f32[512,256]{1,0:T(8,128)S(1)} %collective-permute-done.1.b2, f32[512,256]{1,0:T(8,128)S(1)} %collective-permute-done.2.b3, ...), custom_call_target="tpu_custom_call" | custom-call | tf_op jit(solution)/shard_map/pallas_call | solution.py:323
  60.9 0.5 collective-permute-start.4
  61.4 0.8 %collective-permute-done.4 = f32[16,256]{1,0:T(8,128)S(1)} collective-permute-done((f32[16,256]{1,0:T(8,128)S(1)}, f32[16,256]{1,0:T(8,128)S(1)}, u32[]{:S(2)}, u32[]{:S(2)}) %collective-permute-start.4) | collective-permute-done | bytes 16416 | tf_op jit(solution)/shard_map/ppermute | solution.py:291
  62.2 2.7 %collective-permute-start.7 = (f32[16,256]{1,0:T(8,128)S(1)}, f32[16,256]{1,0:T(8,128)S(1)}, u32[]{:S(2)}, u32[]{:S(2)}) collective-permute-start(f32[16,256]{1,0:T(8,128)S(1)} %add.7.s0), channel_id=1, source_target_pairs={{0,6},{2,4},{4,2},{6,0},{1,7},{3,5},{5,3},{7,1},{8,14},{10,12},{12... | collective-permute-start | bytes 49160 | tf_op jit(solution)/shard_map/ppermute | solution.py:292
  64.9 0.3 collective-permute-start.6
  65.3 0.3 collective-permute-start.5
  65.6 0.5 collective-permute-done.7.s3
  66.1 3.0 %collective-permute-done.6.s2 = f32[16,256]{1,0:T(8,128)S(1)} collective-permute-done((f32[16,256]{1,0:T(8,128)S(1)}, f32[16,256]{1,0:T(8,128)S(1)}, u32[]{:S(2)}, u32[]{:S(2)}) %collective-permute-start.6) | collective-permute-done | bytes 16416 | tf_op jit(solution)/shard_map/ppermute | solution.py:292
  69.0 2.4 %shard_map.54 = (f32[256,1024]{1,0:T(8,128)}, f32[32,256]{1,0:T(8,128)}) custom-call(f32[256,1024]{1,0:T(8,128)S(1)} %copy-done, f32[8,256]{1,0:T(8,128)S(1)} %get-tuple-element.11.m0, f32[4,256,256]{2,1,0:T(8,128)S(1)} %get-tuple-element.15.jumps_in, f32[4,256,256]{2,1,0:T(8,128)S(1)} %get-tuple-element.16.corr_in, f32[16,256]{1,0:T(8,128)S(1)} %add.7.s0, ...), custom_call_target="tpu_custom_call" | custom-call | tf_op jit(solution)/shard_map/pallas_call | solution.py:326
  (11 shorter events, 0.1 us)
Async XLA Ops:
  25.8 8.2 %all-to-all-start.1 = ((f32[4,8,256]{2,1,0:T(8,128)}), f32[4,8,256]{2,1,0:T(8,128)S(1)}, u32[]{:S(2)}, u32[]{:S(2)}) async-start(f32[4,8,256]{2,1,0:T(8,128)} %broadcast_in_dim.9), calls=%async_computation.1 | async-start | bytes 65536 | tf_op jit(solution)/shard_map/all_to_all | solution.py:312
  31.5 27.0 %collective-permute-start.2 = (f32[512,256]{1,0:T(8,128)S(1)}, f32[512,256]{1,0:T(8,128)S(1)}, u32[]{:S(2)}, u32[]{:S(2)}) collective-permute-start(f32[512,256]{1,0:T(8,128)S(1)} %get-tuple-element.13.big.b0), channel_id=1, source_target_pairs={{0,192},{64,0},{128,64},{192,128},{1,193},{65,1},{129,65},{193,129... | collective-permute-start | bytes 1572872 | tf_op jit(solution)/shard_map/ppermute | solution.py:311
  31.6 26.9 %collective-permute-start = (f32[512,256]{1,0:T(8,128)S(1)}, f32[512,256]{1,0:T(8,128)S(1)}, u32[]{:S(2)}, u32[]{:S(2)}) collective-permute-start(f32[512,256]{1,0:T(8,128)S(1)} %get-tuple-element.13.big.b0), channel_id=1, source_target_pairs={{0,64},{64,128},{128,192},{192,0},{1,65},{65,129},{129,193},{193,1... | collective-permute-start | bytes 1572872 | tf_op jit(solution)/shard_map/ppermute | solution.py:311
  34.6 23.9 %collective-permute-start.1 = (f32[512,256]{1,0:T(8,128)S(1)}, f32[512,256]{1,0:T(8,128)S(1)}, u32[]{:S(2)}, u32[]{:S(2)}) collective-permute-start(f32[512,256]{1,0:T(8,128)S(1)} %get-tuple-element.13.big.b0), channel_id=1, source_target_pairs={{0,128},{64,192},{128,0},{192,64},{1,129},{65,193},{129,1},{193,65... | collective-permute-start | bytes 1572872 | tf_op jit(solution)/shard_map/ppermute | solution.py:317
  36.5 5.5 %collective-permute-start.3 = (f32[8,256]{1,0:T(8,128)S(1)}, f32[8,256]{1,0:T(8,128)S(1)}, u32[]{:S(2)}, u32[]{:S(2)}) collective-permute-start(f32[8,256]{1,0:T(8,128)S(1)} %shard_map.52), channel_id=1, source_target_pairs={{0,1},{1,0},{2,3},{3,2},{4,5},{5,4},{6,7},{7,6},{8,9},{9,8},{10,11... | collective-permute-start | bytes 24584 | tf_op jit(solution)/shard_map/ppermute | solution.py:318
  58.5 10.5 %copy-start = (f32[256,1024]{1,0:T(8,128)S(1)}, f32[256,1024]{1,0:T(8,128)}, u32[]{:S(2)}) copy-start(f32[256,1024]{1,0:T(8,128)} %signal.3) | copy-start | bytes 3145732
  60.9 1.3 %collective-permute-start.4 = (f32[16,256]{1,0:T(8,128)S(1)}, f32[16,256]{1,0:T(8,128)S(1)}, u32[]{:S(2)}, u32[]{:S(2)}) collective-permute-start(f32[16,256]{1,0:T(8,128)S(1)} %get-tuple-element.17), channel_id=1, source_target_pairs={{0,1},{1,0},{2,3},{3,2},{4,5},{5,4},{6,7},{7,6},{8,9},{9,8},{10,11... | collective-permute-start | bytes 49160 | tf_op jit(solution)/shard_map/ppermute | solution.py:291
  62.2 3.9 %collective-permute-start.7 = (f32[16,256]{1,0:T(8,128)S(1)}, f32[16,256]{1,0:T(8,128)S(1)}, u32[]{:S(2)}, u32[]{:S(2)}) collective-permute-start(f32[16,256]{1,0:T(8,128)S(1)} %add.7.s0), channel_id=1, source_target_pairs={{0,6},{2,4},{4,2},{6,0},{1,7},{3,5},{5,3},{7,1},{8,14},{10,12},{12... | collective-permute-start | bytes 49160 | tf_op jit(solution)/shard_map/ppermute | solution.py:292
  64.9 4.1 %collective-permute-start.6 = (f32[16,256]{1,0:T(8,128)S(1)}, f32[16,256]{1,0:T(8,128)S(1)}, u32[]{:S(2)}, u32[]{:S(2)}) collective-permute-start(f32[16,256]{1,0:T(8,128)S(1)} %add.7.s0), channel_id=1, source_target_pairs={{0,4},{2,6},{4,0},{6,2},{1,5},{3,7},{5,1},{7,3},{8,12},{10,14},{12... | collective-permute-start | bytes 49160 | tf_op jit(solution)/shard_map/ppermute | solution.py:292
  65.3 3.7 %collective-permute-start.5 = (f32[16,256]{1,0:T(8,128)S(1)}, f32[16,256]{1,0:T(8,128)S(1)}, u32[]{:S(2)}, u32[]{:S(2)}) collective-permute-start(f32[16,256]{1,0:T(8,128)S(1)} %add.7.s0), channel_id=1, source_target_pairs={{0,2},{2,0},{4,6},{6,4},{1,3},{3,1},{5,7},{7,5},{8,10},{10,8},{12,... | collective-permute-start | bytes 49160 | tf_op jit(solution)/shard_map/ppermute | solution.py:292
